TPU v7x, 32 devices: a whole 2x2x4 slice. The times are simulated.
32 devices in a mesh: groups: 1, seq: 8 (over z, y), chan: 2 (over x), sub: 2 (over core).
Axes of the slice: x: 2, y: 2, z: 4, core: 2. Of those that a mesh axis runs over, the one named last changes fastest.
Arguments:
- projections: bfloat16 [3, 256, 131072], P(None, 'chan', ('groups', 'seq', 'sub')), may hold values from -6 to 6
- short_taps: float32 [3, 3, 256], P(None, None, 'chan'), may hold values from -4 to 4
- skip_gain: float32 [256], P('chan'), may hold values from -5 to 5
- filter_spec: bfloat16 [2, 256, 8, 7168], P(None, ('chan', 'seq', 'sub')), may hold values from -18 to 18
- keep_first: int32 [64], replicated, may hold values from 0 to 127, as said below
- keep_second: int32 [112], replicated, may hold values from 0 to 127, as said below
- keep_third: int32 [8], replicated, may hold values from 0 to 15, as said below
- out_weight: bfloat16 [256, 256], P(None, 'chan'), may hold values from -0.375 to 0.375
Outputs:
- mixed_out: bfloat16 [256, 131072], P('chan', ('groups', 'seq', 'sub'))
Inputs may be any that keep to these rules, and one draw needn't show every extreme that they name: `keep_first`: distinct and increasing, always holding 0 and 127. `keep_second`: distinct and increasing, always holding 0 and 127. `keep_third`: distinct and increasing, always holding 0 and 15.
All inputs are finite; a program needn't handle non-finite values.
Results may differ from a plain program's by a relative error of at most 0.011.
Values may be sent and summed in bfloat16 or wider, within the bound.
A program may use at most 128 MiB of HBM per device.

v0:
```python
import math

import jax
import jax.numpy as jnp
from jax import lax
from jax.sharding import PartitionSpec as P

A = 128
B = 128


def passed_along(value, axis, steps):
    count = lax.axis_size(axis)
    leading, last = (max(0, -steps), min(count, count - steps))
    return lax.ppermute(value, axis, [(source, source + steps) for source in range(leading, last)])


def product(form, left, right):
    return jnp.einsum(form, left, right, preferred_element_type=jnp.float32)


def complex_product(form, left, right):
    real = product(form, left[0], right[0]) - product(form, left[1], right[1])
    imag = product(form, left[0], right[1]) + product(form, left[1], right[0])
    return (real, imag)


def rotate(value, turn):
    real = value[0] * turn[0] - value[1] * turn[1]
    imag = value[0] * turn[1] + value[1] * turn[0]
    return (real.astype(jnp.bfloat16), imag.astype(jnp.bfloat16))


def fourier_table(row_index, col_index, length, direction):
    angles = (row_index[:, None] * col_index[None, :] % length).astype(jnp.float32) * (
        2.0 * math.pi / length
    )
    factor = 1.0 / math.sqrt(length)
    return (
        (jnp.cos(angles) * factor).astype(jnp.bfloat16),
        (direction * jnp.sin(angles) * factor).astype(jnp.bfloat16),
    )


def twiddle(counts, length, direction):
    angles = (counts % length).astype(jnp.float32) * (2.0 * math.pi / length)
    return (jnp.cos(angles), direction * jnp.sin(angles))


def spectral_tables(keep_first, keep_second, keep_third, size_a, size_b, size_c):
    full_length = size_a * size_b * size_c
    half_index = jnp.arange(size_a // 2, dtype=jnp.int32)
    index_b = jnp.arange(size_b, dtype=jnp.int32)
    index_c = jnp.arange(size_c, dtype=jnp.int32)
    table_first = fourier_table(keep_first, half_index, size_a, -1.0)
    table_second = fourier_table(keep_second, index_b, size_b, -1.0)
    table_third = fourier_table(keep_third, index_c, size_c, -1.0)
    inverse_first = fourier_table(half_index, keep_first, size_a, 1.0)
    inverse_second = fourier_table(index_b, keep_second, size_b, 1.0)
    inverse_third = fourier_table(index_c, keep_third, size_c, 1.0)
    counts_one = keep_first[:, None] * index_b[None, :]
    turn_one = twiddle(counts_one[:, :, None], size_a * size_b, -1.0)
    undo_one = twiddle(counts_one.T[:, None, :], size_a * size_b, 1.0)
    frequency = keep_first[None, :] + size_a * keep_second[:, None]
    counts_two = frequency[:, :, None] * index_c[None, None, :]
    turn_two = twiddle(counts_two, full_length, -1.0)
    undo_two = twiddle(jnp.transpose(counts_two, (2, 0, 1)), full_length, 1.0)
    return (
        table_first,
        table_second,
        table_third,
        inverse_first,
        inverse_second,
        inverse_third,
        turn_one,
        undo_one,
        turn_two,
        undo_two,
    )


def long_conv(signal_row, spectrum_real, spectrum_imag, tables, size_a, size_b, size_c):
    (
        table_first,
        table_second,
        table_third,
        inverse_first,
        inverse_second,
        inverse_third,
        turn_one,
        undo_one,
        turn_two,
        undo_two,
    ) = tables
    signal = signal_row.reshape(size_a // 2, size_b * size_c)
    count_first = table_first[0].shape[0]
    first_real = jnp.dot(table_first[0], signal, preferred_element_type=jnp.float32).reshape(
        count_first, size_b, size_c
    )
    first_imag = jnp.dot(table_first[1], signal, preferred_element_type=jnp.float32).reshape(
        count_first, size_b, size_c
    )
    section_one = rotate((first_real, first_imag), turn_one)
    section_two = rotate(complex_product("qn,pnc->qpc", table_second, section_one), turn_two)
    summed = complex_product("rc,qpc->rqp", table_third, section_two)
    spectrum = rotate(
        summed, (spectrum_real.astype(jnp.float32), spectrum_imag.astype(jnp.float32))
    )
    back_one = rotate(complex_product("cr,rqp->cqp", inverse_third, spectrum), undo_two)
    back_two = rotate(complex_product("nq,cqp->ncp", inverse_second, back_one), undo_one)
    signal_out = product("mp,ncp->mnc", inverse_first[0], back_two[0]) - product(
        "mp,ncp->mnc", inverse_first[1], back_two[1]
    )
    return signal_out.reshape(-1).astype(jnp.bfloat16)


def on_device(
    projections, short_taps, skip_gain, filter_spec, keep_first, keep_second, keep_third, out_weight
):
    tokens_here = projections.shape[2]
    block_tails = projections[:, :, tokens_here - 2 :]
    before = passed_along(block_tails, ("seq", "sub"), 1)
    extended = jnp.concatenate([before, projections], axis=2).astype(jnp.float32)
    filtered = (
        short_taps[:, 0, :, None] * extended[:, :, 2:]
        + short_taps[:, 1, :, None] * extended[:, :, 1:-1]
        + short_taps[:, 2, :, None] * extended[:, :, :-2]
    )
    gated_values = (filtered[1] * filtered[0]).astype(jnp.bfloat16)
    channel_rows = lax.all_to_all(
        gated_values, ("seq", "sub"), split_axis=0, concat_axis=1, tiled=True
    )
    size_c = 2 * channel_rows.shape[1] // (A * B)
    tables = spectral_tables(keep_first, keep_second, keep_third, A, B, size_c)
    count_one = keep_first.shape[0]
    count_two = keep_second.shape[0]
    count_three = keep_third.shape[0]

    def one_channel(members):
        spec_real = members[1].reshape(count_three, count_two, count_one)
        spec_imag = members[2].reshape(count_three, count_two, count_one)
        return long_conv(members[0], spec_real, spec_imag, tables, A, B, size_c)

    conv_rows = lax.map(one_channel, (channel_rows, filter_spec[0], filter_spec[1]))
    token_major = lax.all_to_all(conv_rows, ("seq", "sub"), split_axis=1, concat_axis=0, tiled=True)
    long_part = token_major.astype(jnp.float32)
    gated_mix = (
        filtered[2] * (long_part + skip_gain[:, None] * gated_values.astype(jnp.float32))
    ).astype(jnp.bfloat16)
    mixed_total = jnp.einsum(
        "de,dt->et",
        out_weight,
        lax.all_gather(gated_mix, "chan", axis=0, tiled=True),
        preferred_element_type=jnp.float32,
    )
    return mixed_total.astype(jnp.bfloat16)


def solution(mesh):
    placed = (
        P(None, "chan", ("groups", "seq", "sub")),
        P(None, None, "chan"),
        P("chan"),
        P(None, ("chan", "seq", "sub"), None, None),
        P(),
        P(),
        P(),
        P(None, "chan"),
    )
    return jax.shard_map(
        on_device,
        mesh=mesh,
        in_specs=placed,
        out_specs=P("chan", ("groups", "seq", "sub")),
        check_vma=False,
    )
```

profile of v0, /device:TPU:0, one launch (start us, length us, event | category | flops | bytes accessed | tf_op | source)
XLA Modules:
  0.0 483.9 jit_solution(17304372457311116088)
XLA Ops:
  6.5 1.0 slice.37
  7.6 2.4 collective-permute-start
  10.9 4.6 maximum_convert_fusion
  15.5 9.2 %fusion.266 = f32[3,128,8192]{2,1,0:T(8,128)} fusion(f32[3,128,8194]{2,1,0:T(8,128)S(1)} %maximum_convert_fusion, f32[3,128]{1,0:T(4,128)S(1)} %get-tuple-element.296, f32[3,128]{1,0:T(4,128)S(1)} %get-tuple-element.297, f32[3,128]{1,0:T(4,128)S(1)} %bitcast.215), kind=kLoop, calls=%fused_computation.296 | loop fusion | flops 15728640 | bytes 50336256 | tf_op jit(solution)/shard_map/add | solution.py:125
  24.7 5.2 %fusion.290 = bf16[16,8,8192]{2,1,0:T(8,128)(2,1)} fusion(f32[3,128,8192]{2,1,0:T(8,128)} %fusion.266), kind=kLoop, calls=%fused_computation.318 | loop fusion | flops 2097152 | bytes 10485760 | tf_op jit(solution)/shard_map/convert_element_type | solution.py:129
  29.9 10.2 %all-to-all-start = ((bf16[16,8,8192]{2,1,0:T(8,128)(2,1)}), bf16[16,8,8192]{2,1,0:T(8,128)(2,1)}, u32[]{:S(2)}, u32[]{:S(2)}) async-start(bf16[16,8,8192]{2,1,0:T(8,128)(2,1)} %fusion.290), calls=%async_computation | async-start | bytes 4194304 | tf_op jit(solution)/shard_map/all_to_all | solution.py:130
  40.3 1.4 slice_bitcast_fusion.1
  41.6 39.6 %all-to-all-done = bf16[16,8,8192]{2,1,0:T(8,128)(2,1)} async-done(((bf16[16,8,8192]{2,1,0:T(8,128)(2,1)}), bf16[16,8,8192]{2,1,0:T(8,128)(2,1)}, u32[]{:S(2)}, u32[]{:S(2)}) %all-to-all-start) | async-done | bytes 2097184 | tf_op jit(solution)/shard_map/all_to_all | solution.py:130
  81.3 266.0 %while.12 = (s32[]{:T(128)}, bf16[8,131072]{1,0:T(8,128)(2,1)}, bf16[8,131072]{1,0:T(8,128)(2,1)}, bf16[8,8,7168]{2,1,0:T(8,128)(2,1)}, bf16[8,8,7168]{2,1,0:T(8...) while((s32[]{:T(128)}, bf16[8,131072]{1,0:T(8,128)(2,1)}, ...), condition=%wide.region_1.2_spmd.clone.clone, body=%wide.region_0.1_spmd.clone.clone.sunk | while | flops 327950336 | bytes 30209400 | solution.py:144
  81.3 3.2 dynamic-slice_reduce_fusion.2
  89.4 2.6 subtract_convert_fusion.13
  92.9 1.0 dynamic-slice_convert_fusion.3
  96.0 2.7 subtract_convert_fusion.15
  101.7 1.1 copy.70
  102.7 1.4 convert_element_type.712
  104.1 10.4 %dynamic_update_slice.7 = bf16[8,131072]{1,0:T(8,128)(2,1)} dynamic-update-slice(bf16[8,131072]{1,0:T(8,128)(2,1)} %get-tuple-element.393, bf16[1,131072]{1,0:T(2,128)(2,1)S(1)} %convert_element_type.712, s32[]{:T(128)} %get-tuple-element.392, s32[]{:T(128)} %constant.130.clone.1..sunk) | dynamic-update-slice | bytes 524292 | tf_op jit(solution)/shard_map/while/body/jit(dynamic_update_index_in_dim)/dynamic_update_slice | solution.py:144
  114.5 3.2 dynamic-slice_reduce_fusion.2
  122.6 2.6 subtract_convert_fusion.13
  129.3 2.7 subtract_convert_fusion.15
  134.9 1.1 copy.70
  136.0 1.4 convert_element_type.712
  137.4 10.4 %dynamic_update_slice.7 = bf16[8,131072]{1,0:T(8,128)(2,1)} dynamic-update-slice(bf16[8,131072]{1,0:T(8,128)(2,1)} %get-tuple-element.393, bf16[1,131072]{1,0:T(2,128)(2,1)S(1)} %convert_element_type.712, s32[]{:T(128)} %get-tuple-element.392, s32[]{:T(128)} %constant.130.clone.1..sunk) | dynamic-update-slice | bytes 524292 | tf_op jit(solution)/shard_map/while/body/jit(dynamic_update_index_in_dim)/dynamic_update_slice | solution.py:144
  147.7 3.2 dynamic-slice_reduce_fusion.2
  155.9 2.6 subtract_convert_fusion.13
  162.5 2.7 subtract_convert_fusion.15
  168.2 1.1 copy.70
  169.2 1.4 convert_element_type.712
  170.6 10.4 %dynamic_update_slice.7 = bf16[8,131072]{1,0:T(8,128)(2,1)} dynamic-update-slice(bf16[8,131072]{1,0:T(8,128)(2,1)} %get-tuple-element.393, bf16[1,131072]{1,0:T(2,128)(2,1)S(1)} %convert_element_type.712, s32[]{:T(128)} %get-tuple-element.392, s32[]{:T(128)} %constant.130.clone.1..sunk) | dynamic-update-slice | bytes 524292 | tf_op jit(solution)/shard_map/while/body/jit(dynamic_update_index_in_dim)/dynamic_update_slice | solution.py:144
  181.0 3.2 dynamic-slice_reduce_fusion.2
  189.2 2.6 subtract_convert_fusion.13
  195.8 2.7 subtract_convert_fusion.15
  201.4 1.1 copy.70
  202.5 1.4 convert_element_type.712
  203.9 10.4 %dynamic_update_slice.7 = bf16[8,131072]{1,0:T(8,128)(2,1)} dynamic-update-slice(bf16[8,131072]{1,0:T(8,128)(2,1)} %get-tuple-element.393, bf16[1,131072]{1,0:T(2,128)(2,1)S(1)} %convert_element_type.712, s32[]{:T(128)} %get-tuple-element.392, s32[]{:T(128)} %constant.130.clone.1..sunk) | dynamic-update-slice | bytes 524292 | tf_op jit(solution)/shard_map/while/body/jit(dynamic_update_index_in_dim)/dynamic_update_slice | solution.py:144
  214.2 3.2 dynamic-slice_reduce_fusion.2
  222.4 2.6 subtract_convert_fusion.13
  225.9 1.0 dynamic-slice_convert_fusion.3
  229.0 2.7 subtract_convert_fusion.15
  234.7 1.1 copy.70
  235.8 1.4 convert_element_type.712
  237.1 10.4 %dynamic_update_slice.7 = bf16[8,131072]{1,0:T(8,128)(2,1)} dynamic-update-slice(bf16[8,131072]{1,0:T(8,128)(2,1)} %get-tuple-element.393, bf16[1,131072]{1,0:T(2,128)(2,1)S(1)} %convert_element_type.712, s32[]{:T(128)} %get-tuple-element.392, s32[]{:T(128)} %constant.130.clone.1..sunk) | dynamic-update-slice | bytes 524292 | tf_op jit(solution)/shard_map/while/body/jit(dynamic_update_index_in_dim)/dynamic_update_slice | solution.py:144
  247.5 3.2 dynamic-slice_reduce_fusion.2
  255.7 2.6 subtract_convert_fusion.13
  262.3 2.7 subtract_convert_fusion.15
  267.9 1.1 copy.70
  269.0 1.4 convert_element_type.712
  270.4 10.4 %dynamic_update_slice.7 = bf16[8,131072]{1,0:T(8,128)(2,1)} dynamic-update-slice(bf16[8,131072]{1,0:T(8,128)(2,1)} %get-tuple-element.393, bf16[1,131072]{1,0:T(2,128)(2,1)S(1)} %convert_element_type.712, s32[]{:T(128)} %get-tuple-element.392, s32[]{:T(128)} %constant.130.clone.1..sunk) | dynamic-update-slice | bytes 524292 | tf_op jit(solution)/shard_map/while/body/jit(dynamic_update_index_in_dim)/dynamic_update_slice | solution.py:144
  280.8 3.2 dynamic-slice_reduce_fusion.2
  288.9 2.6 subtract_convert_fusion.13
  295.6 2.7 subtract_convert_fusion.15
  301.2 1.1 copy.70
  302.3 1.4 convert_element_type.712
  303.6 10.4 %dynamic_update_slice.7 = bf16[8,131072]{1,0:T(8,128)(2,1)} dynamic-update-slice(bf16[8,131072]{1,0:T(8,128)(2,1)} %get-tuple-element.393, bf16[1,131072]{1,0:T(2,128)(2,1)S(1)} %convert_element_type.712, s32[]{:T(128)} %get-tuple-element.392, s32[]{:T(128)} %constant.130.clone.1..sunk) | dynamic-update-slice | bytes 524292 | tf_op jit(solution)/shard_map/while/body/jit(dynamic_update_index_in_dim)/dynamic_update_slice | solution.py:144
  314.0 3.2 dynamic-slice_reduce_fusion.2
  322.2 2.6 subtract_convert_fusion.13
  328.8 2.7 subtract_convert_fusion.15
  334.4 1.1 copy.70
  335.5 1.4 convert_element_type.712
  336.9 10.4 %dynamic_update_slice.7 = bf16[8,131072]{1,0:T(8,128)(2,1)} dynamic-update-slice(bf16[8,131072]{1,0:T(8,128)(2,1)} %get-tuple-element.393, bf16[1,131072]{1,0:T(2,128)(2,1)S(1)} %convert_element_type.712, s32[]{:T(128)} %get-tuple-element.392, s32[]{:T(128)} %constant.130.clone.1..sunk) | dynamic-update-slice | bytes 524292 | tf_op jit(solution)/shard_map/while/body/jit(dynamic_update_index_in_dim)/dynamic_update_slice | solution.py:144
  347.3 58.7 %all_to_all.29 = bf16[8,16,8192]{2,0,1:T(8,128)(2,1)S(1)} all-to-all(bf16[8,16,8192]{2,0,1:T(8,128)(2,1)} %bitcast.214), channel_id=1, replica_groups=mesh['groups'=1,'seq'=8,'chan'=2,'sub'=2] {'seq','sub'}, dimensions={1} | all-to-all | bytes 4194304 | tf_op jit(solution)/shard_map/all_to_all | solution.py:145
  406.0 7.3 %fusion.271 = bf16[128,8192]{1,0:T(8,128)(2,1)} fusion(f32[3,128,8192]{2,1,0:T(8,128)} %fusion.266, bf16[8,16,8192]{2,0,1:T(8,128)(2,1)S(1)} %all_to_all.29, f32[128]{0:T(128)S(1)} %copy-done.5), kind=kLoop, calls=%fused_computation.307 | loop fusion | flops 8388608 | bytes 16777728 | tf_op jit(solution)/shard_map/convert_element_type | solution.py:149
  413.3 57.3 %all-gather.2.cloned.1.call-done = bf16[256,8192]{1,0:T(8,128)(2,1)} async-done(((bf16[128,8192]{1,0:T(8,128)(2,1)}), bf16[256,8192]{1,0:T(8,128)(2,1)}) %all-gather.2.cloned.1.call-update) | async-done | bytes 4194320 | tf_op jit(solution)/shard_map/all_gather | solution.py:153
  470.7 3.5 fusion.268
  474.2 2.9 copy.33
  (267 shorter events, 93.0 us)
Async XLA Ops:
  6.5 464.1 %copy-start = (bf16[256,128]{1,0:T(8,128)(2,1)S(1)}, bf16[256,128]{1,0:T(8,128)(2,1)}, u32[]{:S(2)}) copy-start(bf16[256,128]{1,0:T(8,128)(2,1)} %param.17) | copy-start | bytes 196612
  7.6 3.3 collective-permute-start
  29.9 10.3 %copy-start.3 = (s32[112]{0:T(128)S(1)}, s32[112]{0:T(128)}, u32[]{:S(2)}) copy-start(s32[112]{0:T(128)} %param.15) | copy-start | bytes 1348
  29.9 10.3 %copy-start.4 = (s32[64]{0:T(128)S(1)}, s32[64]{0:T(128)}, u32[]{:S(2)}) copy-start(s32[64]{0:T(128)} %param.14) | copy-start | bytes 772
  29.9 10.4 %copy-start.1 = (bf16[2,8,8,7168]{3,2,1,0:T(8,128)(2,1)S(1)}, bf16[2,8,8,7168]{3,2,1,0:T(8,128)(2,1)}, u32[]{:S(2)}) copy-start(bf16[2,8,8,7168]{3,2,1,0:T(8,128)(2,1)} %param.13) | copy-start | bytes 5505028
  29.9 51.4 %copy-start.2 = (s32[8]{0:T(128)S(1)}, s32[8]{0:T(128)}, u32[]{:S(2)}) copy-start(s32[8]{0:T(128)} %param.16) | copy-start | bytes 100
  29.9 51.4 %all-to-all-start = ((bf16[16,8,8192]{2,1,0:T(8,128)(2,1)}), bf16[16,8,8192]{2,1,0:T(8,128)(2,1)}, u32[]{:S(2)}, u32[]{:S(2)}) async-start(bf16[16,8,8192]{2,1,0:T(8,128)(2,1)} %fusion.290), calls=%async_computation | async-start | bytes 4194304 | tf_op jit(solution)/shard_map/all_to_all | solution.py:130
  40.1 430.5 %all-gather.2.cloned.1.call-start = ((), (), s32[]{:S(2)}) async-start(), calls=%async_computation.2 | async-start | bytes 6291456 | tf_op jit(solution)/shard_map/all_gather | solution.py:153
  347.3 58.7 %copy-start.5 = (f32[128]{0:T(128)S(1)}, f32[128]{0:T(128)}, u32[]{:S(2)}) copy-start(f32[128]{0:T(128)} %param.12) | copy-start | bytes 1540
Sparse Core Ops, SparseCore 0:
  413.4 57.1 all-gather.1
where the time goes:
time: 487 us; the launch traced here: 484 us
  local copies, waits for them, and re-layouts  155 us (32%)
  matrix products  104 us (21%)
  waiting for transfers between devices  97.1 us (20%)
  blocking collectives  58.7 us (12%)
  other arithmetic  41.1 us (8%)
  between operations  13.5 us (3%)
  starting transfers between devices  12.6 us (3%)
    dot_general x144, matrix products, product(): return jnp.einsum(form, left, right, preferred_element_type=jnp.float32)  94.4 us
    dynamic_update_slice x8, local copies, waits for them, and re-layouts, on_device(): lax.map(one_channel, (channel_rows, filter_spec[0], filter_spec[1]))  83 us
    all_to_all x1, blocking collectives, on_device(): lax.all_to_all(conv_rows, ('seq', 'sub'), split_axis=1, concat_axis=0, ti...  58.7 us
    all_gather x1, waiting for transfers between devices, on_device(): lax.all_gather(gated_mix, 'chan', axis=0, tiled=True)  57.3 us
    all_to_all x1, waiting for transfers between devices, on_device(): lax.all_to_all(gated_values, ('seq', 'sub'), split_axis=0, concat_axis=1,...  39.6 us
    dynamic_slice x8, local copies, waits for them, and re-layouts, on_device(): lax.map(one_channel, (channel_rows, filter_spec[0], filter_spec[1]))  25.6 us
    convert_element_type x16, local copies, waits for them, and re-layouts, long_conv(): return signal_out.reshape(-1).astype(jnp.bfloat16)  19.5 us
    all_to_all x1, starting transfers between devices, on_device(): lax.all_to_all(gated_values, ('seq', 'sub'), split_axis=0, concat_axis=1,...  10.2 us
  transfers between devices with their start and end apart: 3, of which 3 were waited for; matrix products, arithmetic and copies ran while one was open for 0% of the time, Pallas kernels for 0%

commit v1 on v0

v1 whole, which is shorter than its diff:
```python
import functools
import math

import jax
import jax.numpy as jnp
from jax import lax
from jax.experimental import pallas as pl
from jax.experimental.pallas import tpu as pltpu
from jax.sharding import PartitionSpec as P

A = 128
B = 128
LANES = 128
SLAB = 16
PARTS = 2


def passed_along(value, axis, steps):
    count = lax.axis_size(axis)
    leading, last = (max(0, -steps), min(count, count - steps))
    return lax.ppermute(value, axis, [(source, source + steps) for source in range(leading, last)])


def fourier_table(row_index, col_index, length, direction):
    angles = (row_index[:, None] * col_index[None, :] % length).astype(jnp.float32) * (
        2.0 * math.pi / length
    )
    factor = 1.0 / math.sqrt(length)
    return (
        (jnp.cos(angles) * factor).astype(jnp.bfloat16),
        (direction * jnp.sin(angles) * factor).astype(jnp.bfloat16),
    )


def twiddle(counts, length, direction):
    angles = (counts % length).astype(jnp.float32) * (2.0 * math.pi / length)
    return (jnp.cos(angles), direction * jnp.sin(angles))


def pad_to(value, axis, size):
    widths = [(0, 0)] * value.ndim
    widths[axis] = (0, size - value.shape[axis])
    return jnp.pad(value, widths)


def slab_kron(table):
    rows, cols = table.shape
    eye = jnp.eye(SLAB, dtype=table.dtype)
    return (table[:, None, :, None] * eye[None, :, None, :]).reshape(rows * SLAB, cols * SLAB)


def conv_tables(keep_first, keep_second, keep_third, size_c, sources, per_source):
    full_length = A * B * size_c
    half = jnp.arange(A // 2, dtype=jnp.int32).reshape(sources, per_source).T.reshape(-1)
    index_b = jnp.arange(B, dtype=jnp.int32)
    index_c = jnp.arange(size_c, dtype=jnp.int32)
    count_one = keep_first.shape[0]
    first = jnp.concatenate(fourier_table(keep_first, half, A, -1.0), axis=0)
    sr, si = (pad_to(part.T, 1, LANES) for part in fourier_table(keep_second, index_b, B, -1.0))
    second = jnp.concatenate(
        [jnp.concatenate([sr, si], axis=1), jnp.concatenate([-si, sr], axis=1)], axis=0
    )
    tr, ti = fourier_table(keep_third, index_c, size_c, -1.0)
    third = jnp.concatenate([slab_kron(tr), slab_kron(ti)], axis=0)
    vr, vi = (slab_kron(part) for part in fourier_table(index_c, keep_third, size_c, 1.0))
    undo_third = jnp.concatenate(
        [jnp.concatenate([vr, -vi], axis=1), jnp.concatenate([vi, vr], axis=1)], axis=0
    )
    ur, ui = (pad_to(part.T, 0, LANES) for part in fourier_table(index_b, keep_second, B, 1.0))
    undo_second = jnp.concatenate(
        [jnp.concatenate([ur, ui], axis=1), jnp.concatenate([-ui, ur], axis=1)], axis=0
    )
    fr, fi = fourier_table(half, keep_first, A, 1.0)
    undo_first = jnp.concatenate([fr, -fi], axis=1)
    turn_one = twiddle(keep_first[:, None] * index_b[None, :], A * B, -1.0)
    k2 = pad_to(keep_second, 0, LANES)
    k1 = keep_first.reshape(count_one // SLAB, 1, SLAB, 1)
    counts_two = (k1 + A * k2) * index_c[None, :, None, None]
    turn_two = twiddle(
        counts_two.reshape(count_one // SLAB, size_c * SLAB, LANES), full_length, -1.0
    )
    return (first, *turn_one, second, *turn_two, third, undo_third, undo_second, undo_first)


def dot(left, right):
    return jnp.dot(left, right, preferred_element_type=jnp.float32)


def conv_kernel(
    size_c,
    x_ref,
    filt_ref,
    first,
    one_re,
    one_im,
    second,
    two_re,
    two_im,
    third,
    undo_third,
    undo_second,
    undo_first,
    out_ref,
    held,
    back,
):
    width = B * size_c
    sources = x_ref.shape[1]
    per_source = x_ref.shape[2] // width
    count_one = one_re.shape[0]
    slabs = count_one // SLAB
    rows = size_c * SLAB
    kept = filt_ref.shape[3]
    x = jnp.concatenate(
        [x_ref[0, :, j * width : (j + 1) * width] for j in range(per_source)], axis=0
    )
    section = dot(first[...], x)
    for n3 in range(size_c):
        lanes = slice(n3 * LANES, (n3 + 1) * LANES)
        re, im = section[:count_one, lanes], section[count_one:, lanes]
        turned_re = (re * one_re[...] - im * one_im[...]).astype(jnp.bfloat16)
        turned_im = (re * one_im[...] + im * one_re[...]).astype(jnp.bfloat16)
        for s in range(slabs):
            at = slice(n3 * SLAB, (n3 + 1) * SLAB)
            held[s, at, :LANES] = turned_re[s * SLAB : (s + 1) * SLAB]
            held[s, at, LANES:] = turned_im[s * SLAB : (s + 1) * SLAB]
    for s in range(slabs):
        value = dot(held[s], second[...])
        re, im = value[:, :LANES], value[:, LANES:]
        tr, ti = two_re[s], two_im[s]
        value = jnp.concatenate([re * tr - im * ti, re * ti + im * tr], axis=1).astype(jnp.bfloat16)
        value = dot(third[...], value)
        re = value[:kept, :LANES] - value[kept:, LANES:]
        im = value[:kept, LANES:] + value[kept:, :LANES]
        hr = filt_ref[0, 0, s].astype(jnp.float32)
        hi = filt_ref[1, 0, s].astype(jnp.float32)
        value = jnp.concatenate([re * hr - im * hi, re * hi + im * hr], axis=0).astype(jnp.bfloat16)
        value = dot(undo_third[...], value)
        re, im = value[:rows], value[rows:]
        value = jnp.concatenate([re * tr + im * ti, im * tr - re * ti], axis=1).astype(jnp.bfloat16)
        value = dot(value, undo_second[...])
        here = slice(s * SLAB, (s + 1) * SLAB)
        there = slice(count_one + s * SLAB, count_one + (s + 1) * SLAB)
        ur, ui = one_re[here], one_im[here]
        for n3 in range(size_c):
            lanes = slice(n3 * LANES, (n3 + 1) * LANES)
            re = value[n3 * SLAB : (n3 + 1) * SLAB, :LANES]
            im = value[n3 * SLAB : (n3 + 1) * SLAB, LANES:]
            back[here, lanes] = (re * ur + im * ui).astype(jnp.bfloat16)
            back[there, lanes] = (im * ur - re * ui).astype(jnp.bfloat16)
    result = dot(undo_first[...], back[...]).astype(jnp.bfloat16)
    for j in range(per_source):
        out_ref[0, :, j * width : (j + 1) * width] = result[j * sources : (j + 1) * sources]


def whole_block(array):
    zeros = (0,) * array.ndim
    return pl.BlockSpec(array.shape, lambda d: zeros)


def convolve(rows, filt, tables, size_c):
    channels, sources, tokens = rows.shape
    _, _, slabs, kept, _ = filt.shape
    count_one = slabs * SLAB
    return pl.pallas_call(
        functools.partial(conv_kernel, size_c),
        out_shape=jax.ShapeDtypeStruct(rows.shape, jnp.bfloat16),
        grid=(channels,),
        in_specs=[
            pl.BlockSpec((1, sources, tokens), lambda d: (d, 0, 0)),
            pl.BlockSpec((2, 1, slabs, kept, LANES), lambda d: (0, d, 0, 0, 0)),
        ]
        + [whole_block(table) for table in tables],
        out_specs=pl.BlockSpec((1, sources, tokens), lambda d: (d, 0, 0)),
        scratch_shapes=[
            pltpu.VMEM((slabs, size_c * SLAB, 2 * LANES), jnp.bfloat16),
            pltpu.VMEM((2 * count_one, B * size_c), jnp.bfloat16),
        ],
        compiler_params=pltpu.CompilerParams(vmem_limit_bytes=56 * 2**20),
        cost_estimate=pl.CostEstimate(
            flops=channels * 400_000_000, bytes_accessed=8 * 2**20, transcendentals=0
        ),
        name="spectral_conv",
    )(rows, filt, *tables)


def order_matrix(size_c):
    width = B * size_c
    row = lax.broadcasted_iota(jnp.int32, (width, width), 0)
    col = lax.broadcasted_iota(jnp.int32, (width, width), 1)
    return (col == row % size_c * B + row // size_c).astype(jnp.bfloat16)


def reordered(value, order, size_c, back):
    width = B * size_c
    if order is None:
        split = (size_c, B) if back else (B, size_c)
        shaped = value.reshape(value.shape[0], -1, *split)
        return jnp.swapaxes(shaped, 2, 3).reshape(value.shape)
    form = "dw,vw->dv" if back else "dv,vw->dw"
    pieces = [
        jnp.einsum(
            form, value[:, at : at + width], order, preferred_element_type=jnp.float32
        ).astype(jnp.bfloat16)
        for at in range(0, value.shape[1], width)
    ]
    return jnp.concatenate(pieces, axis=1)


def on_device(
    projections, short_taps, skip_gain, filter_spec, keep_first, keep_second, keep_third, out_weight
):
    tokens_here = projections.shape[2]
    ring = ("seq", "sub")
    sources = lax.axis_size(ring)
    channels = projections.shape[1] // sources
    size_c = 2 * tokens_here * sources // (A * B)
    width = B * size_c
    per_source = tokens_here // width
    count_one, count_two, count_three = (
        keep_first.shape[0],
        keep_second.shape[0],
        keep_third.shape[0],
    )
    order = order_matrix(size_c) if width <= 4096 else None

    before = passed_along(projections[:, :, tokens_here - 2 :], ring, 1)
    extended = jnp.concatenate([before, projections], axis=2).astype(jnp.float32)
    filtered = (
        short_taps[:, 0, :, None] * extended[:, :, 2:]
        + short_taps[:, 1, :, None] * extended[:, :, 1:-1]
        + short_taps[:, 2, :, None] * extended[:, :, :-2]
    )
    gated_values = (filtered[1] * filtered[0]).astype(jnp.bfloat16)

    outgoing = reordered(gated_values, order, size_c, False)
    received = lax.all_to_all(
        outgoing.reshape(sources, channels, tokens_here), ring, split_axis=0, concat_axis=0
    )
    rows = jnp.swapaxes(received, 0, 1)

    filt = filter_spec.reshape(2, channels, count_three, count_two, count_one // SLAB, SLAB)
    filt = pad_to(jnp.transpose(filt, (0, 1, 4, 2, 5, 3)), 5, LANES)
    filt = filt.reshape(2, channels, count_one // SLAB, count_three * SLAB, LANES)
    tables = conv_tables(keep_first, keep_second, keep_third, size_c, sources, per_source)
    conv_rows = convolve(rows, filt, tables, size_c)

    conv_out = jnp.swapaxes(conv_rows, 0, 1)
    parts = PARTS if per_source % PARTS == 0 else 1
    step = tokens_here // parts
    mixed = []
    for part in range(parts):
        span = slice(part * step, (part + 1) * step)
        returned = lax.all_to_all(conv_out[:, :, span], ring, split_axis=0, concat_axis=0)
        token_major = reordered(returned.reshape(sources * channels, step), order, size_c, True)
        gated_mix = (
            filtered[2][:, span]
            * (
                token_major.astype(jnp.float32)
                + skip_gain[:, None] * gated_values[:, span].astype(jnp.float32)
            )
        ).astype(jnp.bfloat16)
        gathered = lax.all_gather(gated_mix, "chan", axis=0, tiled=True)
        mixed.append(
            jnp.einsum(
                "de,dt->et", out_weight, gathered, preferred_element_type=jnp.float32
            ).astype(jnp.bfloat16)
        )
    return jnp.concatenate(mixed, axis=1)


def solution(mesh):
    placed = (
        P(None, "chan", ("groups", "seq", "sub")),
        P(None, None, "chan"),
        P("chan"),
        P(None, ("chan", "seq", "sub"), None, None),
        P(),
        P(),
        P(),
        P(None, "chan"),
    )
    return jax.shard_map(
        on_device,
        mesh=mesh,
        in_specs=placed,
        out_specs=P("chan", ("groups", "seq", "sub")),
        check_vma=False,
    )
```

time: 487 us -> 298 us (0.61)
  local copies, waits for them, and re-layouts: 155 us -> 51.3 us
  matrix products: 104 us -> 34 us
  blocking collectives: 58.7 us -> 0 us
  Pallas kernels: 0 us -> 27.4 us
  starting transfers between devices: 12.6 us -> 23.2 us
    dynamic_update_slice x8 -> x0, local copies, waits for them, and re-layouts: 83 us -> none  [on_device(): lax.map(one_channel, (channel_rows, filter_spec[0], filter_spec[1]))]
    dot_general x161 -> x10, matrix products: 104 us -> 34 us  [the longest x8 29.3 us: reordered(): jnp.einsum(form, value[:, at:at + width], order, preferred_element_type=j...]
    all_to_all x1 -> x0, blocking collectives: 58.7 us -> none  [on_device(): lax.all_to_all(conv_rows, ('seq', 'sub'), split_axis=1, concat_axis=0, ti...]
    convert_element_type x65 -> x0, local copies, waits for them, and re-layouts: 36.9 us -> none  [the longest x16 19.5 us: long_conv(): return signal_out.reshape(-1).astype(jnp.bfloat16)]
    pallas_call x0 -> x1, Pallas kernels: none -> 27.4 us  [convolve(): pl.pallas_call(functools.partial(conv_kernel, size_c), out_shape=jax.Shap...]
    dynamic_slice x8 -> x0, local copies, waits for them, and re-layouts: 25.6 us -> none  [on_device(): lax.map(one_channel, (channel_rows, filter_spec[0], filter_spec[1]))]
    unnamed x14 -> x25, local copies, waits for them, and re-layouts: 0.03 us -> 18.2 us
    convert_element_type x17 -> x7, other arithmetic: 18.1 us -> 3.14 us  [the longest x1 2.02 us: on_device(): gated_mix = (filtered[2][:, span] * (token_major.astype(jnp.float32) + sk...]
  transfers between devices with their start and end apart: 3 -> 6, of which waited for: 3 -> 4; matrix products, arithmetic and copies ran while one was open for 0% -> 23% of each run, Pallas kernels for 0% -> 0%
where the time goes in v1:
time: 298 us; the launch traced here: 293 us
  waiting for transfers between devices  101 us (34%)
  local copies, waits for them, and re-layouts  51.3 us (17%)
  other arithmetic  42.2 us (14%)
  matrix products  34 us (11%)
  Pallas kernels  27.4 us (9%)
  starting transfers between devices  23.2 us (8%)
  between operations  14.2 us (5%)
    all_gather x2, waiting for transfers between devices, on_device(): gathered = lax.all_gather(gated_mix, 'chan', axis=0, tiled=True)  67 us
    all_to_all x2, waiting for transfers between devices, on_device(): lax.all_to_all(conv_out[:, :, span], ring, split_axis=0, concat_axis=0)  33.1 us
    dot_general x8, matrix products, reordered(): jnp.einsum(form, value[:, at:at + width], order, preferred_element_type=j...  29.3 us
    pallas_call x1, Pallas kernels, convolve(): pl.pallas_call(functools.partial(conv_kernel, size_c), out_shape=jax.Shap...  27.4 us
    unnamed x25, local copies, waits for them, and re-layouts  18.2 us
    all_to_all x2, starting transfers between devices, on_device(): lax.all_to_all(conv_out[:, :, span], ring, split_axis=0, concat_axis=0)  13 us
    reshape x1, local copies, waits for them, and re-layouts, on_device(): filter_spec.reshape(2, channels, count_three, count_two, count_one // SLA...  12.8 us
    add x1, other arithmetic, on_device(): short_taps[:, 0, :, None] * extended[:, :, 2:]  9.36 us
  transfers between devices with their start and end apart: 6, of which 4 were waited for; matrix products, arithmetic and copies ran while one was open for 23% of the time, Pallas kernels for 0%

profile of v1, /device:TPU:0, one launch (start us, length us, event | category | flops | bytes accessed | tf_op | source)
XLA Modules:
  0.0 293.1 jit_solution(4840020589758323810)
XLA Ops:
  6.5 1.0 slice.74
  7.6 2.4 collective-permute-start
  10.0 0.8 fusion.71
  10.8 5.7 %add_compare_fusion = pred[2048,2048]{1,0:T(32,128)(4,1)} fusion(s32[2048]{0:T(1024)S(1)} %get-tuple-element.39, s32[2048]{0:T(1024)S(1)} %get-tuple-element.42, s32[2048]{0:T(1024)S(1)} %get-tuple-element.40, s32[2048]{0:T(1024)S(1)} %get-tuple-element.41, pred[2048]{0:T(1024)(128)(4,1)S(1)} %get-tuple-element.43, pred[2048]{0:T(1024)(128)(4,1)S(1)} %get-tuple-element.44), kind=kLoop, calls=%fused_computation | loop fusion | flops 20971520 | bytes 4231168 | tf_op jit(solution)/shard_map/eq | solution.py:191
  16.5 4.6 %maximum_convert_fusion = f32[3,128,8194]{2,1,0:T(8,128)S(1)} fusion(bf16[3,128,8192]{2,1,0:T(8,128)(2,1)} %param.8, bf16[3,128,2]{2,1,0:T(8,128)(2,1)S(1)} %collective-permute-done), kind=kLoop, calls=%fused_computation.6 | loop fusion | flops 12585984 | bytes 18878976 | tf_op jit(solution)/shard_map/convert_element_type | solution.py:228
  21.1 9.4 %fusion = f32[3,128,8192]{2,1,0:T(8,128)} fusion(f32[3,128,8194]{2,1,0:T(8,128)S(1)} %maximum_convert_fusion, f32[3,128]{1,0:T(4,128)S(1)} %get-tuple-element.37, f32[3,128]{1,0:T(4,128)S(1)} %get-tuple-element.38, f32[3,128]{1,0:T(4,128)S(1)} %bitcast.73), kind=kLoop, calls=%fused_computation.2 | loop fusion | flops 15728640 | bytes 50336256 | tf_op jit(solution)/shard_map/add | solution.py:230
  30.5 7.7 %fusion.5 = (bf16[128,8192]{1,0:T(8,128)(2,1)S(1)}, f32[128,8192]{1,0:T(8,128)}) fusion(f32[3,128,8192]{2,1,0:T(8,128)} %fusion), kind=kLoop, calls=%fused_computation.22 | loop fusion | flops 2097152 | bytes 18874368 | tf_op jit(solution)/shard_map/convert_element_type | solution.py:234
  38.2 2.5 convolution_convert_fusion.6
  40.7 2.5 convolution_convert_fusion.7
  43.3 2.5 convolution_convert_fusion.8
  45.8 2.5 convolution_convert_fusion.9
  48.4 1.5 maximum_bitcast_fusion
  49.8 7.5 %all-to-all-start = ((bf16[16,8,8192]{2,1,0:T(8,128)(2,1)}), bf16[16,8,8192]{2,1,0:T(8,128)(2,1)}, u32[]{:S(2)}, u32[]{:S(2)}) async-start(bf16[16,8,8192]{2,1,0:T(8,128)(2,1)} %maximum_bitcast_fusion), calls=%async_computation | async-start | bytes 4194304 | tf_op jit(solution)/shard_map/all_to_all | solution.py:237
  57.3 12.8 %reshape.214 = bf16[2,8,8,112,4,16]{5,4,3,2,1,0:T(4,128)(2,1)} reshape(bf16[2,8,8,7168]{3,2,1,0:T(8,128)(2,1)} %param.11) | data formatting | bytes 3670016 | tf_op jit(solution)/shard_map/reshape | solution.py:242
  70.1 18.2 %copy.24 = bf16[2,8,4,8,16,112]{5,4,3,2,1,0:T(8,128)(2,1)} copy(bf16[2,8,4,8,16,112]{4,2,5,3,1,0:T(4,128)(2,1)} %bitcast.67) | data formatting | bytes 3670016
  88.3 0.1 reshape.219
  88.4 3.7 %pad.22.clone = bf16[2,8,4,8,16,128]{5,4,3,2,1,0:T(8,128)(2,1)} pad(bf16[2,8,4,8,16,112]{5,4,3,2,1,0:T(8,128)(2,1)} %copy.24, bf16[]{:T(256)} %constant.130.clone.1), padding=0_0x0_0x0_0x0_0x0_0x0_16 | pad | bytes 3932162 | tf_op jit(solution)/shard_map/jit(_pad)/pad | solution.py:43
  92.1 0.3 multiply_convert_fusion
  92.4 0.1 mul.456
  92.5 0.1 add.166
  92.5 0.1 multiply_convert_fusion.11
  92.7 0.1 broadcast_multiply_fusion.3
  92.8 0.5 mul.477
  93.3 0.5 mul.472
  93.7 0.1 multiply_convert_fusion.8
  93.8 0.1 broadcast_multiply_fusion
  94.0 0.3 mul.487
  94.3 0.3 mul.491
  94.7 0.3 multiply_convert_fusion.2
  95.0 0.1 broadcast_add_fusion
  95.1 3.2 %sine_multiply_fusion = (f32[4,256,128]{2,1,0:T(8,128)}, f32[4,256,128]{2,1,0:T(8,128)}) fusion(s32[256]{0:T(256)S(1)} %mul.456, s32[4,16,128]{2,1,0:T(8,128)S(1)} %broadcast_add_fusion), kind=kLoop, calls=%fused_computation.47 | loop fusion | flops 1966080 | bytes 1082368 | tf_op jit(solution)/shard_map/mul | solution.py:37
  98.3 0.2 fusion.46
  98.5 0.3 multiply_convert_fusion.5
  98.9 0.7 pad_maximum_fusion.3.undo_first
  99.6 0.6 pad_maximum_fusion.2.first
  100.2 0.7 pad_maximum_fusion.1.third
  100.9 0.7 maximum_maximum_fusion.1.second
  101.5 0.7 maximum_maximum_fusion.2.undo_second
  102.2 0.7 maximum_maximum_fusion.undo_third
  102.9 0.8 sine_multiply_fusion.1
  103.7 4.1 %copy.29 = bf16[16,8,8192]{2,0,1:T(8,128)(2,1)} copy(bf16[16,8,8192]{2,1,0:T(8,128)(2,1)} %all-to-all-done) | data formatting | bytes 4194304 | tf_op jit(solution)/shard_map/all_to_all | solution.py:237
  107.8 27.4 %spectral_conv.1 = bf16[8,16,8192]{2,1,0:T(8,128)(2,1)} custom-call(bf16[8,16,8192]{2,1,0:T(8,128)(2,1)} %bitcast.69, bf16[2,8,4,128,128]{4,3,2,1,0:T(8,128)(2,1)} %bitcast.68, bf16[128,64]{1,0:T(8,128)(2,1)} %pad_maximum_fusion.2.first, f32[64,128]{1,0:T(8,128)} %get-tuple-element.36.one_re, f32[64,128]{1,0:T(8,128)} %get-tuple-element.35.one_im, ...), custom_call_target="tpu_custom_call" | custom-call | flops 3200000000 | bytes 8388608 | tf_op jit(solution)/shard_map/spectral_conv/pallas_call | solution.py:165
  135.2 1.7 fusion.68
  136.9 1.6 copy.18
  138.4 6.2 %all-to-all-start.1 = ((bf16[16,8,4096]{2,1,0:T(8,128)(2,1)}), bf16[16,8,4096]{2,1,0:T(8,128)(2,1)}, u32[]{:S(2)}, u32[]{:S(2)}) async-start(bf16[16,8,4096]{2,1,0:T(8,128)(2,1)} %copy.18), calls=%async_computation.1 | async-start | bytes 2097152 | tf_op jit(solution)/shard_map/all_to_all | solution.py:254
  144.6 1.5 copy.19
  146.2 21.4 %all-to-all-done.1 = bf16[16,8,4096]{2,1,0:T(8,128)(2,1)} async-done(((bf16[16,8,4096]{2,1,0:T(8,128)(2,1)}), bf16[16,8,4096]{2,1,0:T(8,128)(2,1)}, u32[]{:S(2)}, u32[]{:S(2)}) %all-to-all-start.1) | async-done | bytes 1048608 | tf_op jit(solution)/shard_map/all_to_all | solution.py:254
  167.6 6.9 %all-to-all-start.2 = ((bf16[16,8,4096]{2,1,0:T(8,128)(2,1)}), bf16[16,8,4096]{2,1,0:T(8,128)(2,1)S(1)}, u32[]{:S(2)}, u32[]{:S(2)}) async-start(bf16[16,8,4096]{2,1,0:T(8,128)(2,1)} %copy.19), calls=%async_computation.2 | async-start | bytes 2097152 | tf_op jit(solution)/shard_map/all_to_all | solution.py:254
  174.5 0.3 all-gather.5.cloned.1.call-start
  174.8 6.2 %convolution_convert_fusion.4 = bf16[128,2048]{1,0:T(8,128)(2,1)} fusion(pred[2048,2048]{1,0:T(32,128)(4,1)} %add_compare_fusion, bf16[128,4096]{1,0:T(8,128)(2,1)} %bitcast.8), kind=kOutput, calls=%fused_computation.16 | convolution fusion | flops 1074003968 | bytes 5242880 | tf_op jit(solution)/shard_map/dw,vw->dv/dot_general | solution.py:202
  181.0 4.8 %convolution_convert_fusion.5 = bf16[128,2048]{1,0:T(8,128)(2,1)} fusion(pred[2048,2048]{1,0:T(32,128)(4,1)S(1)} %copy-done.3, bf16[128,4096]{1,0:T(8,128)(2,1)} %bitcast.8), kind=kOutput, calls=%fused_computation.17 | convolution fusion | flops 1074003968 | bytes 5242880 | tf_op jit(solution)/shard_map/dw,vw->dv/dot_general | solution.py:202
  185.8 11.7 %all-to-all-done.2 = bf16[16,8,4096]{2,1,0:T(8,128)(2,1)S(1)} async-done(((bf16[16,8,4096]{2,1,0:T(8,128)(2,1)}), bf16[16,8,4096]{2,1,0:T(8,128)(2,1)S(1)}, u32[]{:S(2)}, u32[]{:S(2)}) %all-to-all-start.2) | async-done | bytes 1048608 | tf_op jit(solution)/shard_map/all_to_all | solution.py:254
  197.4 5.2 %convolution_convert_fusion.2 = bf16[128,2048]{1,0:T(8,128)(2,1)S(1)} fusion(pred[2048,2048]{1,0:T(32,128)(4,1)} %add_compare_fusion, bf16[128,4096]{1,0:T(8,128)(2,1)S(1)} %bitcast.71), kind=kOutput, calls=%fused_computation.14 | convolution fusion | flops 1074003968 | bytes 5242880 | tf_op jit(solution)/shard_map/dw,vw->dv/dot_general | solution.py:202
  202.7 2.9 convolution_convert_fusion.3
  205.7 2.0 fusion.7
  207.7 0.0 all-gather.5.cloned.1.call-update
  207.8 0.0 all-gather.3.cloned.1.call-start
  207.8 0.7 all-gather.3.cloned.1.call-update
  208.5 34.7 %all-gather.5.cloned.1.call-done = bf16[256,4096]{1,0:T(8,128)(2,1)} async-done(((bf16[128,4096]{1,0:T(8,128)(2,1)}), bf16[256,4096]{1,0:T(8,128)(2,1)}) %all-gather.5.cloned.1.call-update) | async-done | bytes 2097168 | tf_op jit(solution)/shard_map/all_gather | solution.py:263
  243.2 2.4 fusion.3
  245.6 32.3 %all-gather.3.cloned.1.call-done = bf16[256,4096]{1,0:T(8,128)(2,1)} async-done(((bf16[128,4096]{1,0:T(8,128)(2,1)}), bf16[256,4096]{1,0:T(8,128)(2,1)}) %all-gather.3.cloned.1.call-update) | async-done | bytes 2097168 | tf_op jit(solution)/shard_map/all_gather | solution.py:263
  277.9 2.4 fusion.2
  280.3 1.5 pad_maximum_fusion
  281.7 4.1 %copy.20 = bf16[128,8192]{1,0:T(8,128)(2,1)} copy(bf16[128,8192]{0,1:T(8,128)(2,1)} %pad_maximum_fusion) | data formatting | bytes 4194304 | tf_op jit(solution)/shard_map/concatenate | solution.py:269
  (37 shorter events, 0.2 us)
Async XLA Ops:
  6.5 236.7 %copy-start = (bf16[256,128]{1,0:T(8,128)(2,1)S(1)}, bf16[256,128]{1,0:T(8,128)(2,1)}, u32[]{:S(2)}) copy-start(bf16[256,128]{1,0:T(8,128)(2,1)} %param.15) | copy-start | bytes 196612
  7.6 8.9 %collective-permute-start = (bf16[3,128,2]{2,1,0:T(8,128)(2,1)S(1)}, bf16[3,128,2]{2,1,0:T(8,128)(2,1)S(1)}, u32[]{:S(2)}, u32[]{:S(2)}) collective-permute-start(bf16[3,128,2]{2,1,0:T(8,128)(2,1)S(1)} %slice.74), channel_id=1, source_target_pairs={{0,1},{1,4},{4,5},{5,8},{8,9},{9,12},{12,13},{13,16},{16,17},{17,2... | collective-permute-start | bytes 4616 | tf_op jit(solution)/shard_map/ppermute | solution.py:21
  30.5 7.7 %copy-start.2 = (pred[2048,2048]{1,0:T(32,128)(4,1)S(1)}, pred[2048,2048]{1,0:T(32,128)(4,1)}, u32[]{:S(2)}) copy-start(pred[2048,2048]{1,0:T(32,128)(4,1)} %add_compare_fusion) | copy-start | bytes 12582916
  49.8 53.9 %all-to-all-start = ((bf16[16,8,8192]{2,1,0:T(8,128)(2,1)}), bf16[16,8,8192]{2,1,0:T(8,128)(2,1)}, u32[]{:S(2)}, u32[]{:S(2)}) async-start(bf16[16,8,8192]{2,1,0:T(8,128)(2,1)} %maximum_bitcast_fusion), calls=%async_computation | async-start | bytes 4194304 | tf_op jit(solution)/shard_map/all_to_all | solution.py:237
  88.3 3.8 %copy-start.8 = (s32[112]{0:T(128)S(1)}, s32[112]{0:T(128)}, u32[]{:S(2)}) copy-start(s32[112]{0:T(128)} %param.13) | copy-start | bytes 1348
  88.3 4.2 %copy-start.7 = (s32[64]{0:T(128)S(1)}, s32[64]{0:T(128)}, u32[]{:S(2)}) copy-start(s32[64]{0:T(128)} %param.12) | copy-start | bytes 772
  88.3 4.3 %copy-start.9 = (s32[8]{0:T(128)S(1)}, s32[8]{0:T(128)}, u32[]{:S(2)}) copy-start(s32[8]{0:T(128)} %param.14) | copy-start | bytes 100
  138.4 29.2 %all-to-all-start.1 = ((bf16[16,8,4096]{2,1,0:T(8,128)(2,1)}), bf16[16,8,4096]{2,1,0:T(8,128)(2,1)}, u32[]{:S(2)}, u32[]{:S(2)}) async-start(bf16[16,8,4096]{2,1,0:T(8,128)(2,1)} %copy.18), calls=%async_computation.1 | async-start | bytes 2097152 | tf_op jit(solution)/shard_map/all_to_all | solution.py:254
  167.6 29.8 %all-to-all-start.2 = ((bf16[16,8,4096]{2,1,0:T(8,128)(2,1)}), bf16[16,8,4096]{2,1,0:T(8,128)(2,1)S(1)}, u32[]{:S(2)}, u32[]{:S(2)}) async-start(bf16[16,8,4096]{2,1,0:T(8,128)(2,1)} %copy.19), calls=%async_computation.2 | async-start | bytes 2097152 | tf_op jit(solution)/shard_map/all_to_all | solution.py:254
  174.5 68.7 %all-gather.5.cloned.1.call-start = ((), (), s32[]{:S(2)}) async-start(), calls=%async_computation.4 | async-start | bytes 3145728 | tf_op jit(solution)/shard_map/all_gather | solution.py:263
  174.8 6.2 %copy-start.3 = (pred[2048,2048]{1,0:T(32,128)(4,1)S(1)}, pred[2048,2048]{1,0:T(32,128)(4,1)}, u32[]{:S(2)}) copy-start(pred[2048,2048]{1,0:T(32,128)(4,1)} %add_compare_fusion) | copy-start | bytes 12582916
  197.4 5.3 %copy-start.4 = (pred[2048,2048]{1,0:T(32,128)(4,1)S(1)}, pred[2048,2048]{1,0:T(32,128)(4,1)}, u32[]{:S(2)}) copy-start(pred[2048,2048]{1,0:T(32,128)(4,1)} %add_compare_fusion) | copy-start | bytes 12582916
  202.7 3.0 %copy-start.1 = (f32[128,8192]{1,0:T(8,128)S(1)}, f32[128,8192]{1,0:T(8,128)}, u32[]{:S(2)}) copy-start(f32[128,8192]{1,0:T(8,128)} %get-tuple-element.6) | copy-start | bytes 12582916
  202.7 3.0 %copy-start.5 = (bf16[128,2048]{1,0:T(8,128)(2,1)S(1)}, bf16[128,2048]{1,0:T(8,128)(2,1)}, u32[]{:S(2)}) copy-start(bf16[128,2048]{1,0:T(8,128)(2,1)} %convolution_convert_fusion.4) | copy-start | bytes 1572868
  202.7 3.0 %copy-start.6 = (bf16[128,2048]{1,0:T(8,128)(2,1)S(1)}, bf16[128,2048]{1,0:T(8,128)(2,1)}, u32[]{:S(2)}) copy-start(bf16[128,2048]{1,0:T(8,128)(2,1)} %convolution_convert_fusion.5) | copy-start | bytes 1572868
  202.7 3.0 %copy-start.10 = (f32[128]{0:T(128)S(1)}, f32[128]{0:T(128)}, u32[]{:S(2)}) copy-start(f32[128]{0:T(128)} %param.10) | copy-start | bytes 1540
  207.8 70.1 %all-gather.3.cloned.1.call-start = ((), (), s32[]{:S(2)}) async-start(), calls=%async_computation.3 | async-start | bytes 3145728 | tf_op jit(solution)/shard_map/all_gather | solution.py:263
Sparse Core Ops, SparseCore 0:
  207.9 35.2 all-gather.4
  244.7 33.1 all-gather.2

commit v2 on v1

--- a/solution.py
+++ b/solution.py
@@ -186,25 +186,117 @@
 
 def order_matrix(size_c):
     width = B * size_c
-    row = lax.broadcasted_iota(jnp.int32, (width, width), 0)
-    col = lax.broadcasted_iota(jnp.int32, (width, width), 1)
-    return (col == row % size_c * B + row // size_c).astype(jnp.bfloat16)
-
-
-def reordered(value, order, size_c, back):
-    width = B * size_c
-    if order is None:
-        split = (size_c, B) if back else (B, size_c)
-        shaped = value.reshape(value.shape[0], -1, *split)
-        return jnp.swapaxes(shaped, 2, 3).reshape(value.shape)
-    form = "dw,vw->dv" if back else "dv,vw->dw"
-    pieces = [
-        jnp.einsum(
-            form, value[:, at : at + width], order, preferred_element_type=jnp.float32
-        ).astype(jnp.bfloat16)
-        for at in range(0, value.shape[1], width)
+    col = jnp.arange(width, dtype=jnp.int32)
+    origin = jnp.swapaxes(col.reshape(B, size_c), 0, 1).reshape(-1)
+    return (col[:, None] == origin[None, :]).astype(jnp.bfloat16)
+
+
+def short_filter(taps, which, before, block):
+    extended = jnp.concatenate([before, block], axis=1).astype(jnp.float32)
+    at = 3 * which
+    total = taps[:, at : at + 1] * extended[:, LANES:]
+    total += taps[:, at + 1 : at + 2] * pltpu.roll(extended, 1, 1)[:, LANES:]
+    return total + taps[:, at + 2 : at + 3] * pltpu.roll(extended, 2, 1)[:, LANES:]
+
+
+def head_kernel(halo, taps, order, ahead, block, gated_ref, sent_ref):
+    first = pl.program_id(0) == 0
+    filtered = [
+        short_filter(taps, p, jnp.where(first, halo[p], ahead[p]), block[p]) for p in range(2)
     ]
-    return jnp.concatenate(pieces, axis=1)
+    gated = (filtered[1] * filtered[0]).astype(jnp.bfloat16)
+    gated_ref[...] = gated
+    sent_ref[...] = dot(gated, order[...]).astype(jnp.bfloat16)
+
+
+def head(projections, halo, taps, order):
+    _, channels, tokens = projections.shape
+    width = order.shape[0]
+    per_block = width // LANES
+    block = pl.BlockSpec((channels, width), lambda j: (0, j))
+    shape = jax.ShapeDtypeStruct((channels, tokens), jnp.bfloat16)
+    return pl.pallas_call(
+        head_kernel,
+        out_shape=(shape, shape),
+        grid=(tokens // width,),
+        in_specs=[
+            whole_block(halo),
+            whole_block(taps),
+            whole_block(order),
+            pl.BlockSpec(
+                (2, channels, LANES), lambda j: (0, 0, jnp.maximum(j * per_block - 1, 0))
+            ),
+            pl.BlockSpec((2, channels, width), lambda j: (0, 0, j)),
+        ],
+        out_specs=(block, block),
+        compiler_params=pltpu.CompilerParams(vmem_limit_bytes=56 * 2**20),
+        cost_estimate=pl.CostEstimate(
+            flops=2 * channels * tokens * width, bytes_accessed=16 * 2**20, transcendentals=0
+        ),
+        name="gate_and_reorder",
+    )(halo, taps, order, projections, projections)
+
+
+def tail_kernel(base, halo, taps, skip, order, ahead, block, gated, returned, out_ref):
+    first = pl.program_id(0) + base == 0
+    filtered = short_filter(taps, 2, jnp.where(first, halo[2], ahead[0]), block[0])
+    conv = lax.dot_general(
+        returned[...], order[...], (((1,), (1,)), ((), ())), preferred_element_type=jnp.float32
+    )
+    mix = filtered * (conv + skip[...] * gated[...].astype(jnp.float32))
+    out_ref[...] = mix.astype(jnp.bfloat16)
+
+
+def tail(projections, halo, taps, skip, order, gated, returned, base):
+    channels, tokens = returned.shape
+    width = order.shape[0]
+    per_block = width // LANES
+    return pl.pallas_call(
+        functools.partial(tail_kernel, base),
+        out_shape=jax.ShapeDtypeStruct((channels, tokens), jnp.bfloat16),
+        grid=(tokens // width,),
+        in_specs=[
+            whole_block(halo),
+            whole_block(taps),
+            whole_block(skip),
+            whole_block(order),
+            pl.BlockSpec(
+                (1, channels, LANES),
+                lambda j: (2, 0, jnp.maximum((j + base) * per_block - 1, 0)),
+            ),
+            pl.BlockSpec((1, channels, width), lambda j: (2, 0, j + base)),
+            pl.BlockSpec((channels, width), lambda j: (0, j + base)),
+            pl.BlockSpec((channels, width), lambda j: (0, j)),
+        ],
+        out_specs=pl.BlockSpec((channels, width), lambda j: (0, j)),
+        compiler_params=pltpu.CompilerParams(vmem_limit_bytes=56 * 2**20),
+        cost_estimate=pl.CostEstimate(
+            flops=2 * channels * tokens * width, bytes_accessed=12 * 2**20, transcendentals=0
+        ),
+        name="reorder_and_mix",
+    )(halo, taps, skip, order, projections, projections, gated, returned)
+
+
+def project(out_weight, gated_mix):
+    count = lax.axis_size("chan")
+    me = lax.axis_index("chan")
+    depth = gated_mix.shape[0]
+    held = [gated_mix] + [
+        lax.ppermute(gated_mix, "chan", [(i, (i + k) % count) for i in range(count)])
+        for k in range(1, count)
+    ]
+    total = 0.0
+    for k, value in enumerate(held):
+        owner = (me - k + count) % count
+        weight = lax.dynamic_slice_in_dim(out_weight, owner * depth, depth, 0)
+        total += jnp.einsum("de,dt->et", weight, value, preferred_element_type=jnp.float32)
+    return total.astype(jnp.bfloat16)
+
+
+def reordered(value, size_c, back):
+    split = (size_c, B) if back else (B, size_c)
+    shaped = value.reshape(value.shape[0], -1, *split)
+    return jnp.swapaxes(shaped, 2, 3).reshape(value.shape)
 
 
 def on_device(
@@ -225,15 +317,19 @@
     order = order_matrix(size_c) if width <= 4096 else None
 
     before = passed_along(projections[:, :, tokens_here - 2 :], ring, 1)
-    extended = jnp.concatenate([before, projections], axis=2).astype(jnp.float32)
-    filtered = (
-        short_taps[:, 0, :, None] * extended[:, :, 2:]
-        + short_taps[:, 1, :, None] * extended[:, :, 1:-1]
-        + short_taps[:, 2, :, None] * extended[:, :, :-2]
-    )
-    gated_values = (filtered[1] * filtered[0]).astype(jnp.bfloat16)
-
-    outgoing = reordered(gated_values, order, size_c, False)
+    if order is None:
+        extended = jnp.concatenate([before, projections], axis=2).astype(jnp.float32)
+        filtered = (
+            short_taps[:, 0, :, None] * extended[:, :, 2:]
+            + short_taps[:, 1, :, None] * extended[:, :, 1:-1]
+            + short_taps[:, 2, :, None] * extended[:, :, :-2]
+        )
+        gated_values = (filtered[1] * filtered[0]).astype(jnp.bfloat16)
+        outgoing = reordered(gated_values, size_c, False)
+    else:
+        halo = jnp.pad(before, ((0, 0), (0, 0), (LANES - 2, 0)))
+        taps = short_taps.reshape(9, -1).T
+        gated_values, outgoing = head(projections, halo, taps, order)
     received = lax.all_to_all(
         outgoing.reshape(sources, channels, tokens_here), ring, split_axis=0, concat_axis=0
     )
@@ -252,20 +348,28 @@
     for part in range(parts):
         span = slice(part * step, (part + 1) * step)
         returned = lax.all_to_all(conv_out[:, :, span], ring, split_axis=0, concat_axis=0)
-        token_major = reordered(returned.reshape(sources * channels, step), order, size_c, True)
-        gated_mix = (
-            filtered[2][:, span]
-            * (
-                token_major.astype(jnp.float32)
-                + skip_gain[:, None] * gated_values[:, span].astype(jnp.float32)
+        returned = returned.reshape(sources * channels, step)
+        if order is None:
+            token_major = reordered(returned, size_c, True)
+            gated_mix = (
+                filtered[2][:, span]
+                * (
+                    token_major.astype(jnp.float32)
+                    + skip_gain[:, None] * gated_values[:, span].astype(jnp.float32)
+                )
+            ).astype(jnp.bfloat16)
+        else:
+            gated_mix = tail(
+                projections,
+                halo,
+                taps,
+                skip_gain[:, None],
+                order,
+                gated_values,
+                returned,
+                part * (step // width),
             )
-        ).astype(jnp.bfloat16)
-        gathered = lax.all_gather(gated_mix, "chan", axis=0, tiled=True)
-        mixed.append(
-            jnp.einsum(
-                "de,dt->et", out_weight, gathered, preferred_element_type=jnp.float32
-            ).astype(jnp.bfloat16)
-        )
+        mixed.append(project(out_weight, gated_mix))
     return jnp.concatenate(mixed, axis=1)
 
 

time: 298 us -> 214 us (0.72)
  waiting for transfers between devices: 101 us -> 54.4 us
  Pallas kernels: 27.4 us -> 63.2 us
  matrix products: 34 us -> 1.9 us
  other arithmetic: 42.2 us -> 18.8 us
  between operations: 14.2 us -> 0.23 us
  local copies, waits for them, and re-layouts: 51.3 us -> 48.1 us
    all_gather x2 -> x0, waiting for transfers between devices: 67 us -> none  [on_device(): gathered = lax.all_gather(gated_mix, 'chan', axis=0, tiled=True)]
    pallas_call x0 -> x3, Pallas kernels: none -> 35.8 us  [the longest x2 22.1 us: tail(): pl.pallas_call(functools.partial(tail_kernel, base), out_shape=jax.ShapeD...]
    dot_general x10 -> x4, matrix products: 34 us -> 1.9 us  [project(): jnp.einsum('de,dt->et', weight, value, preferred_element_type=jnp.float32)]
    ppermute x0 -> x2, waiting for transfers between devices: none -> 23.4 us  [project(): lax.ppermute(gated_mix, 'chan', [(i, (i + k) % count) for i in range(coun...]
    add x2 -> x0, other arithmetic: 9.37 us -> none  [the longest x1 9.36 us: on_device(): short_taps[:, 0, :, None] * extended[:, :, 2:]]
    convert_element_type x3 -> x1, other arithmetic: 14.3 us -> 7.43 us  [order_matrix(): return (col[:, None] == origin[None, :]).astype(jnp.bfloat16)]
    eq x1 -> x0, other arithmetic: 5.71 us -> none  [order_matrix(): return (col == row % size_c * B + row // size_c).astype(jnp.bfloat16)]
    concatenate x1 -> x0, local copies, waits for them, and re-layouts: 4.06 us -> none  [on_device(): return jnp.concatenate(mixed, axis=1)]
  transfers between devices with their start and end apart: 6 -> 6, of which waited for: 4 -> 4; matrix products, arithmetic and copies ran while one was open for 23% -> 27% of each run, Pallas kernels for 0% -> 10%
where the time goes in v2:
time: 214 us; the launch traced here: 212 us
  Pallas kernels  63.2 us (30%)
  waiting for transfers between devices  54.4 us (25%)
  local copies, waits for them, and re-layouts  48.1 us (22%)
  starting transfers between devices  25.4 us (12%)
  other arithmetic  18.8 us (9%)
    all_to_all x2, waiting for transfers between devices, on_device(): lax.all_to_all(conv_out[:, :, span], ring, split_axis=0, concat_axis=0)  31 us
    pallas_call x1, Pallas kernels, convolve(): pl.pallas_call(functools.partial(conv_kernel, size_c), out_shape=jax.Shap...  27.4 us
    ppermute x2, waiting for transfers between devices, project(): lax.ppermute(gated_mix, 'chan', [(i, (i + k) % count) for i in range(coun...  23.4 us
    pallas_call x2, Pallas kernels, tail(): pl.pallas_call(functools.partial(tail_kernel, base), out_shape=jax.ShapeD...  22.1 us
    unnamed x21, local copies, waits for them, and re-layouts  19.2 us
    pallas_call x1, Pallas kernels, head(): pl.pallas_call(head_kernel, out_shape=(shape, shape), grid=(tokens // wid...  13.8 us
    all_to_all x2, starting transfers between devices, on_device(): lax.all_to_all(conv_out[:, :, span], ring, split_axis=0, concat_axis=0)  12.9 us
    reshape x1, local copies, waits for them, and re-layouts, on_device(): filter_spec.reshape(2, channels, count_three, count_two, count_one // SLA...  12.8 us
  transfers between devices with their start and end apart: 6, of which 4 were waited for; matrix products, arithmetic and copies ran while one was open for 27% of the time, Pallas kernels for 10%

profile of v2, /device:TPU:0, one launch (start us, length us, event | category | flops | bytes accessed | tf_op | source)
XLA Modules:
  0.0 212.0 jit_solution(539370567519390728)
XLA Ops:
  0.0 0.0 copy-start
  0.0 1.0 slice.9
  1.0 2.4 %collective-permute-start = (bf16[3,128,2]{2,1,0:T(8,128)(2,1)S(1)}, bf16[3,128,2]{2,1,0:T(8,128)(2,1)S(1)}, u32[]{:S(2)}, u32[]{:S(2)}) collective-permute-start(bf16[3,128,2]{2,1,0:T(8,128)(2,1)S(1)} %slice.9), channel_id=1, source_target_pairs={{0,1},{1,4},{4,5},{5,8},{8,9},{9,12},{12,13},{13,16},{16,17},{17,2... | collective-permute-start | bytes 4616 | tf_op jit(solution)/shard_map/ppermute | solution.py:21
  3.4 0.0 copy-start.6
  3.4 7.4 %fusion.order = bf16[2048,2048]{1,0:T(8,128)(2,1)} fusion(s32[2048]{0:T(1024)S(1)} %add_bitcast_fusion), kind=kLoop, calls=%fused_computation.1 | loop fusion | flops 8388608 | bytes 8396800 | tf_op jit(solution)/shard_map/convert_element_type | solution.py:191
  10.9 0.0 copy-done.6
  10.9 0.7 copy.22
  11.6 0.0 collective-permute-done
  11.6 0.7 pad.26.halo
  12.4 13.8 %gate_and_reorder.1 = (bf16[128,8192]{1,0:T(8,128)(2,1)}, bf16[128,8192]{1,0:T(8,128)(2,1)}) custom-call(bf16[3,128,128]{2,1,0:T(8,128)(2,1)} %pad.26.halo, f32[128,9]{1,0:T(8,128)} %bitcast.54, bf16[2048,2048]{1,0:T(8,128)(2,1)} %fusion.order, bf16[3,128,8192]{2,1,0:T(8,128)(2,1)} %block.5, bf16[3,128,8192]{2,1,0:T(8,128)(2,1)} %block.5), custom_call_target="tpu_custom_call" | custom-call | flops 4294967296 | bytes 16777216 | tf_op jit(solution)/shard_map/gate_and_reorder/pallas_call | solution.py:218
  26.1 7.2 %all-to-all-start = ((bf16[16,8,8192]{2,1,0:T(8,128)(2,1)}), bf16[16,8,8192]{2,1,0:T(8,128)(2,1)S(1)}, u32[]{:S(2)}, u32[]{:S(2)}) async-start(bf16[16,8,8192]{2,1,0:T(8,128)(2,1)} %bitcast.50), calls=%async_computation | async-start | bytes 4194304 | tf_op jit(solution)/shard_map/all_to_all | solution.py:333
  33.3 12.8 %reshape.254 = bf16[2,8,8,112,4,16]{5,4,3,2,1,0:T(4,128)(2,1)} reshape(bf16[2,8,8,7168]{3,2,1,0:T(8,128)(2,1)} %param.11) | data formatting | bytes 3670016 | tf_op jit(solution)/shard_map/reshape | solution.py:338
  46.1 18.2 %copy.29 = bf16[2,8,4,8,16,112]{5,4,3,2,1,0:T(8,128)(2,1)} copy(bf16[2,8,4,8,16,112]{4,2,5,3,1,0:T(4,128)(2,1)} %bitcast.47) | data formatting | bytes 3670016
  64.3 3.7 %pad.27.clone = bf16[2,8,4,8,16,128]{5,4,3,2,1,0:T(8,128)(2,1)} pad(bf16[2,8,4,8,16,112]{5,4,3,2,1,0:T(8,128)(2,1)} %copy.29, bf16[]{:T(256)} %constant.133.clone.1), padding=0_0x0_0x0_0x0_0x0_0x0_16 | pad | bytes 3932162 | tf_op jit(solution)/shard_map/jit(_pad)/pad | solution.py:43
  68.0 0.1 reshape.259
  68.1 0.0 copy-done.7
  68.1 0.3 multiply_convert_fusion
  68.4 0.1 mul.379
  68.5 0.1 add.156
  68.6 0.1 multiply_convert_fusion.11
  68.7 0.1 broadcast_multiply_fusion.3
  68.8 0.5 mul.400
  69.3 0.5 mul.395
  69.8 0.1 multiply_convert_fusion.8
  69.8 0.1 broadcast_multiply_fusion
  70.0 0.3 mul.410
  70.3 0.3 mul.414
  70.7 0.3 multiply_convert_fusion.2
  71.0 0.1 broadcast_add_fusion
  71.1 3.2 %sine_multiply_fusion = (f32[4,256,128]{2,1,0:T(8,128)}, f32[4,256,128]{2,1,0:T(8,128)}) fusion(s32[256]{0:T(256)S(1)} %mul.379, s32[4,16,128]{2,1,0:T(8,128)S(1)} %broadcast_add_fusion), kind=kLoop, calls=%fused_computation.17 | loop fusion | flops 1966080 | bytes 1082368 | tf_op jit(solution)/shard_map/mul | solution.py:37
  74.3 0.2 fusion.39
  74.6 0.3 multiply_convert_fusion.5
  74.9 0.7 pad_maximum_fusion.3.undo_first
  75.6 0.6 pad_maximum_fusion.2.first
  76.2 0.7 pad_maximum_fusion.1.third
  76.9 0.7 maximum_maximum_fusion.1.second
  77.6 0.7 maximum_maximum_fusion.2.undo_second
  78.3 0.7 maximum_maximum_fusion.undo_third
  79.0 0.9 sine_multiply_fusion.1
  79.8 0.0 all-to-all-done
  79.8 2.5 %copy.31 = bf16[16,8,8192]{2,0,1:T(8,128)(2,1)} copy(bf16[16,8,8192]{2,1,0:T(8,128)(2,1)S(1)} %all-to-all-done) | data formatting | bytes 4194304 | tf_op jit(solution)/shard_map/all_to_all | solution.py:333
  82.3 27.4 %spectral_conv.1 = bf16[8,16,8192]{2,1,0:T(8,128)(2,1)} custom-call(bf16[8,16,8192]{2,1,0:T(8,128)(2,1)} %bitcast.52, bf16[2,8,4,128,128]{4,3,2,1,0:T(8,128)(2,1)} %bitcast.51, bf16[128,64]{1,0:T(8,128)(2,1)} %pad_maximum_fusion.2.first, f32[64,128]{1,0:T(8,128)} %get-tuple-element.33.one_re, f32[64,128]{1,0:T(8,128)} %get-tuple-element.32.one_im, ...), custom_call_target="tpu_custom_call" | custom-call | flops 3200000000 | bytes 8388608 | tf_op jit(solution)/shard_map/spectral_conv/pallas_call | solution.py:165
  109.7 1.7 fusion.59
  111.4 1.6 copy.27
  112.9 6.0 %all-to-all-start.2 = ((bf16[16,8,4096]{2,1,0:T(8,128)(2,1)}), bf16[16,8,4096]{2,1,0:T(8,128)(2,1)S(1)}, u32[]{:S(2)}, u32[]{:S(2)}) async-start(bf16[16,8,4096]{2,1,0:T(8,128)(2,1)} %copy.27), calls=%async_computation.2 | async-start | bytes 2097152 | tf_op jit(solution)/shard_map/all_to_all | solution.py:350
  118.9 0.0 copy-start.9
  118.9 1.5 copy.25
  120.5 21.4 %all-to-all-done.2 = bf16[16,8,4096]{2,1,0:T(8,128)(2,1)S(1)} async-done(((bf16[16,8,4096]{2,1,0:T(8,128)(2,1)}), bf16[16,8,4096]{2,1,0:T(8,128)(2,1)S(1)}, u32[]{:S(2)}, u32[]{:S(2)}) %all-to-all-start.2) | async-done | bytes 1048608 | tf_op jit(solution)/shard_map/all_to_all | solution.py:350
  141.9 6.9 %all-to-all-start.1 = ((bf16[16,8,4096]{2,1,0:T(8,128)(2,1)}), bf16[16,8,4096]{2,1,0:T(8,128)(2,1)S(1)}, u32[]{:S(2)}, u32[]{:S(2)}) async-start(bf16[16,8,4096]{2,1,0:T(8,128)(2,1)} %copy.25), calls=%async_computation.1 | async-start | bytes 2097152 | tf_op jit(solution)/shard_map/all_to_all | solution.py:350
  148.8 0.7 copy.26.skip
  149.5 11.0 %reorder_and_mix.3 = bf16[128,4096]{1,0:T(8,128)(2,1)} custom-call(bf16[3,128,128]{2,1,0:T(8,128)(2,1)} %pad.26.halo, f32[128,9]{1,0:T(8,128)} %bitcast.55, f32[128,1]{1,0:T(8,128)} %copy.26.skip, bf16[2048,2048]{1,0:T(8,128)(2,1)} %fusion.order, bf16[3,128,8192]{2,1,0:T(8,128)(2,1)} %block.5, bf16[3,128,8192]{2,1,0:T(8,128)(2,1)} %block.5, ...), custom_call_target="tpu_custom_call" | custom-call | flops 2147483648 | bytes 12582912 | tf_op jit(solution)/shard_map/reorder_and_mix/pallas_call | solution.py:254
  160.5 1.5 collective-permute-start.2
  162.0 9.7 %all-to-all-done.1 = bf16[16,8,4096]{2,1,0:T(8,128)(2,1)S(1)} async-done(((bf16[16,8,4096]{2,1,0:T(8,128)(2,1)}), bf16[16,8,4096]{2,1,0:T(8,128)(2,1)S(1)}, u32[]{:S(2)}, u32[]{:S(2)}) %all-to-all-start.1) | async-done | bytes 1048608 | tf_op jit(solution)/shard_map/all_to_all | solution.py:350
  171.7 1.0 copy-done.3
  172.7 11.0 %reorder_and_mix.2 = bf16[128,4096]{1,0:T(8,128)(2,1)} custom-call(bf16[3,128,128]{2,1,0:T(8,128)(2,1)} %pad.26.halo, f32[128,9]{1,0:T(8,128)} %bitcast.56, f32[128,1]{1,0:T(8,128)} %copy.26.skip, bf16[2048,2048]{1,0:T(8,128)(2,1)} %fusion.order, bf16[3,128,8192]{2,1,0:T(8,128)(2,1)} %block.5, bf16[3,128,8192]{2,1,0:T(8,128)(2,1)} %block.5, ...), custom_call_target="tpu_custom_call" | custom-call | flops 2147483648 | bytes 12582912 | tf_op jit(solution)/shard_map/reorder_and_mix/pallas_call | solution.py:254
  183.7 1.5 collective-permute-start.1
  185.2 1.0 collective-permute-done.2
  186.2 0.5 fusion.33
  186.7 0.5 fusion.2
  187.2 0.0 copy-start.2
  187.2 22.4 %collective-permute-done.1 = bf16[128,4096]{1,0:T(8,128)(2,1)S(1)} collective-permute-done((bf16[128,4096]{1,0:T(8,128)(2,1)}, bf16[128,4096]{1,0:T(8,128)(2,1)S(1)}, u32[]{:S(2)}, u32[]{:S(2)}) %collective-permute-start.1) | collective-permute-done | bytes 1048608 | tf_op jit(solution)/shard_map/ppermute | solution.py:285
  209.6 0.5 fusion.35
  210.1 0.5 fusion.1
  210.5 1.5 pad_maximum_fusion
  (23 shorter events, 0.1 us)
Async XLA Ops:
  0.0 186.2 %copy-start = (bf16[256,128]{1,0:T(8,128)(2,1)S(1)}, bf16[256,128]{1,0:T(8,128)(2,1)}, u32[]{:S(2)}) copy-start(bf16[256,128]{1,0:T(8,128)(2,1)} %param.15) | copy-start | bytes 196612
  1.0 10.6 %collective-permute-start = (bf16[3,128,2]{2,1,0:T(8,128)(2,1)S(1)}, bf16[3,128,2]{2,1,0:T(8,128)(2,1)S(1)}, u32[]{:S(2)}, u32[]{:S(2)}) collective-permute-start(bf16[3,128,2]{2,1,0:T(8,128)(2,1)S(1)} %slice.9), channel_id=1, source_target_pairs={{0,1},{1,4},{4,5},{5,8},{8,9},{9,12},{12,13},{13,16},{16,17},{17,2... | collective-permute-start | bytes 4616 | tf_op jit(solution)/shard_map/ppermute | solution.py:21
  3.4 7.4 %copy-start.6 = (f32[3,3,128]{2,1,0:T(4,128)S(1)}, f32[3,3,128]{2,1,0:T(4,128)}, u32[]{:S(2)}) copy-start(f32[3,3,128]{2,1,0:T(4,128)} %param.9) | copy-start | bytes 13828
  26.1 53.7 %all-to-all-start = ((bf16[16,8,8192]{2,1,0:T(8,128)(2,1)}), bf16[16,8,8192]{2,1,0:T(8,128)(2,1)S(1)}, u32[]{:S(2)}, u32[]{:S(2)}) async-start(bf16[16,8,8192]{2,1,0:T(8,128)(2,1)} %bitcast.50), calls=%async_computation | async-start | bytes 4194304 | tf_op jit(solution)/shard_map/all_to_all | solution.py:333
  64.3 3.8 %copy-start.7 = (s32[112]{0:T(128)S(1)}, s32[112]{0:T(128)}, u32[]{:S(2)}) copy-start(s32[112]{0:T(128)} %param.13) | copy-start | bytes 1348
  64.3 4.2 %copy-start.5 = (s32[64]{0:T(128)S(1)}, s32[64]{0:T(128)}, u32[]{:S(2)}) copy-start(s32[64]{0:T(128)} %param.12) | copy-start | bytes 772
  64.3 4.3 %copy-start.8 = (s32[8]{0:T(128)S(1)}, s32[8]{0:T(128)}, u32[]{:S(2)}) copy-start(s32[8]{0:T(128)} %param.14) | copy-start | bytes 100
  112.9 28.9 %all-to-all-start.2 = ((bf16[16,8,4096]{2,1,0:T(8,128)(2,1)}), bf16[16,8,4096]{2,1,0:T(8,128)(2,1)S(1)}, u32[]{:S(2)}, u32[]{:S(2)}) async-start(bf16[16,8,4096]{2,1,0:T(8,128)(2,1)} %copy.27), calls=%async_computation.2 | async-start | bytes 2097152 | tf_op jit(solution)/shard_map/all_to_all | solution.py:350
  118.9 29.8 %copy-start.9 = (f32[128]{0:T(128)S(1)}, f32[128]{0:T(128)}, u32[]{:S(2)}) copy-start(f32[128]{0:T(128)} %param.10) | copy-start | bytes 1540
  141.9 7.6 %copy-start.4 = (bf16[16,8,4096]{2,1,0:T(8,128)(2,1)}, bf16[16,8,4096]{2,1,0:T(8,128)(2,1)S(1)}, u32[]{:S(2)}) copy-start(bf16[16,8,4096]{2,1,0:T(8,128)(2,1)S(1)} %all-to-all-done.2) | copy-start | bytes 3145732
  141.9 29.8 %all-to-all-start.1 = ((bf16[16,8,4096]{2,1,0:T(8,128)(2,1)}), bf16[16,8,4096]{2,1,0:T(8,128)(2,1)S(1)}, u32[]{:S(2)}, u32[]{:S(2)}) async-start(bf16[16,8,4096]{2,1,0:T(8,128)(2,1)} %copy.25), calls=%async_computation.1 | async-start | bytes 2097152 | tf_op jit(solution)/shard_map/all_to_all | solution.py:350
  160.5 25.7 %collective-permute-start.2 = (bf16[128,4096]{1,0:T(8,128)(2,1)}, bf16[128,4096]{1,0:T(8,128)(2,1)S(1)}, u32[]{:S(2)}, u32[]{:S(2)}) collective-permute-start(bf16[128,4096]{1,0:T(8,128)(2,1)} %reorder_and_mix.3), channel_id=1, source_target_pairs={{0,2},{2,0},{1,3},{3,1},{4,6},{6,4},{5,7},{7,5},{8,10},{10,8},{9,1... | collective-permute-start | bytes 3145736 | tf_op jit(solution)/shard_map/ppermute | solution.py:285
  171.7 1.0 copy-start.3
  183.7 3.0 %copy-start.1 = (bf16[128,4096]{1,0:T(8,128)(2,1)S(1)}, bf16[128,4096]{1,0:T(8,128)(2,1)}, u32[]{:S(2)}) copy-start(bf16[128,4096]{1,0:T(8,128)(2,1)} %reorder_and_mix.3) | copy-start | bytes 3145732
  183.7 25.9 %collective-permute-start.1 = (bf16[128,4096]{1,0:T(8,128)(2,1)}, bf16[128,4096]{1,0:T(8,128)(2,1)S(1)}, u32[]{:S(2)}, u32[]{:S(2)}) collective-permute-start(bf16[128,4096]{1,0:T(8,128)(2,1)} %reorder_and_mix.2), channel_id=1, source_target_pairs={{0,2},{2,0},{1,3},{3,1},{4,6},{6,4},{5,7},{7,5},{8,10},{10,8},{9,1... | collective-permute-start | bytes 3145736 | tf_op jit(solution)/shard_map/ppermute | solution.py:285
  187.2 22.8 %copy-start.2 = (bf16[128,4096]{1,0:T(8,128)(2,1)S(1)}, bf16[128,4096]{1,0:T(8,128)(2,1)}, u32[]{:S(2)}) copy-start(bf16[128,4096]{1,0:T(8,128)(2,1)} %reorder_and_mix.2) | copy-start | bytes 3145732

commit v3 on v2

--- a/solution.py
+++ b/solution.py
@@ -12,7 +12,7 @@
 B = 128
 LANES = 128
 SLAB = 16
-PARTS = 2
+PARTS = 4
 
 
 def passed_along(value, axis, steps):
@@ -199,42 +199,54 @@
     return total + taps[:, at + 2 : at + 3] * pltpu.roll(extended, 2, 1)[:, LANES:]
 
 
-def head_kernel(halo, taps, order, ahead, block, gated_ref, sent_ref):
-    first = pl.program_id(0) == 0
-    filtered = [
-        short_filter(taps, p, jnp.where(first, halo[p], ahead[p]), block[p]) for p in range(2)
-    ]
-    gated = (filtered[1] * filtered[0]).astype(jnp.bfloat16)
-    gated_ref[...] = gated
-    sent_ref[...] = dot(gated, order[...]).astype(jnp.bfloat16)
+def head_kernel(halo, taps, order, block, gated_ref, sent_ref, held):
+    step = pl.program_id(0)
+    width, columns = order.shape
+    channels = block.shape[1]
+    pieces = block.shape[2] // width
+
+    @pl.when(step == 0)
+    def _():
+        for j in range(pieces):
+            at = j * width
+            filtered = []
+            for p in range(2):
+                before = halo[p] if j == 0 else block[p, :, at - LANES : at]
+                filtered.append(short_filter(taps, p, before, block[p, :, at : at + width]))
+            gated = (filtered[1] * filtered[0]).astype(jnp.bfloat16)
+            gated_ref[:, at : at + width] = gated
+            held[j * channels : (j + 1) * channels] = gated
+
+    moved = dot(held[...], order[...]).astype(jnp.bfloat16)
+    for j in range(pieces):
+        lanes = pl.ds(pl.multiple_of(j * width + step * columns, LANES), columns)
+        sent_ref[:, lanes] = moved[j * channels : (j + 1) * channels]
 
 
 def head(projections, halo, taps, order):
     _, channels, tokens = projections.shape
     width = order.shape[0]
-    per_block = width // LANES
-    block = pl.BlockSpec((channels, width), lambda j: (0, j))
+    columns = width // 4
+    block = pl.BlockSpec((channels, tokens), lambda c: (0, 0))
     shape = jax.ShapeDtypeStruct((channels, tokens), jnp.bfloat16)
     return pl.pallas_call(
         head_kernel,
         out_shape=(shape, shape),
-        grid=(tokens // width,),
+        grid=(width // columns,),
         in_specs=[
             whole_block(halo),
             whole_block(taps),
-            whole_block(order),
-            pl.BlockSpec(
-                (2, channels, LANES), lambda j: (0, 0, jnp.maximum(j * per_block - 1, 0))
-            ),
-            pl.BlockSpec((2, channels, width), lambda j: (0, 0, j)),
+            pl.BlockSpec((width, columns), lambda c: (0, c)),
+            pl.BlockSpec((2, channels, tokens), lambda c: (0, 0, 0)),
         ],
         out_specs=(block, block),
+        scratch_shapes=[pltpu.VMEM((tokens // width * channels, width), jnp.bfloat16)],
         compiler_params=pltpu.CompilerParams(vmem_limit_bytes=56 * 2**20),
         cost_estimate=pl.CostEstimate(
             flops=2 * channels * tokens * width, bytes_accessed=16 * 2**20, transcendentals=0
         ),
         name="gate_and_reorder",
-    )(halo, taps, order, projections, projections)
+    )(halo, taps, order, projections)
 
 
 def tail_kernel(base, halo, taps, skip, order, ahead, block, gated, returned, out_ref):
@@ -345,9 +357,13 @@
     parts = PARTS if per_source % PARTS == 0 else 1
     step = tokens_here // parts
     mixed = []
+    ready = []
     for part in range(parts):
         span = slice(part * step, (part + 1) * step)
-        returned = lax.all_to_all(conv_out[:, :, span], ring, split_axis=0, concat_axis=0)
+        leaving = conv_out[:, :, span]
+        if part >= 2:
+            leaving, _ = lax.optimization_barrier((leaving, ready[part - 2]))
+        returned = lax.all_to_all(leaving, ring, split_axis=0, concat_axis=0)
         returned = returned.reshape(sources * channels, step)
         if order is None:
             token_major = reordered(returned, size_c, True)
@@ -369,7 +385,8 @@
                 returned,
                 part * (step // width),
             )
-        mixed.append(project(out_weight, gated_mix))
+        ready.append(gated_mix)
+    mixed = [project(out_weight, gated_mix) for gated_mix in ready]
     return jnp.concatenate(mixed, axis=1)
 
 

time: 214 us -> 216 us (level)
  waiting for transfers between devices: 54.4 us -> 37.8 us
  Pallas kernels: 63.2 us -> 72.8 us
  starting transfers between devices: 25.4 us -> 32.9 us
    ppermute x2 -> x4, waiting for transfers between devices: 23.4 us -> 11.9 us  [project(): lax.ppermute(gated_mix, 'chan', [(i, (i + k) % count) for i in range(coun...]
    pallas_call x2 -> x4, Pallas kernels: 22.1 us -> 30.6 us  [tail(): pl.pallas_call(functools.partial(tail_kernel, base), out_shape=jax.ShapeD...]
    all_to_all x2 -> x4, starting transfers between devices: 12.9 us -> 18.3 us  [on_device(): returned = lax.all_to_all(leaving, ring, split_axis=0, concat_axis=0)]
    all_to_all x2 -> x4, waiting for transfers between devices: 31 us -> 25.9 us  [on_device(): returned = lax.all_to_all(leaving, ring, split_axis=0, concat_axis=0)]
    optimization_barrier x0 -> x2, local copies, waits for them, and re-layouts: none -> 2.18 us  [on_device(): leaving, _ = lax.optimization_barrier((leaving, ready[part - 2]))]
    ppermute x2 -> x4, starting transfers between devices: 2.99 us -> 5.07 us  [project(): lax.ppermute(gated_mix, 'chan', [(i, (i + k) % count) for i in range(coun...]
    unnamed x21 -> x29, local copies, waits for them, and re-layouts: 19.2 us -> 19 us
  transfers between devices with their start and end apart: 6 -> 10, of which waited for: 4 -> 5; matrix products, arithmetic and copies ran while one was open for 27% -> 28% of each run, Pallas kernels for 10% -> 14%
where the time goes in v3:
time: 216 us; the launch traced here: 215 us
  Pallas kernels  72.8 us (34%)
  local copies, waits for them, and re-layouts  49.2 us (23%)
  waiting for transfers between devices  37.8 us (17%)
  starting transfers between devices  32.9 us (15%)
  other arithmetic  18.9 us (9%)
  matrix products  2.61 us (1%)
    pallas_call x4, Pallas kernels, tail(): pl.pallas_call(functools.partial(tail_kernel, base), out_shape=jax.ShapeD...  30.6 us
    pallas_call x1, Pallas kernels, convolve(): pl.pallas_call(functools.partial(conv_kernel, size_c), out_shape=jax.Shap...  27.4 us
    all_to_all x4, waiting for transfers between devices, on_device(): returned = lax.all_to_all(leaving, ring, split_axis=0, concat_axis=0)  25.9 us
    unnamed x29, local copies, waits for them, and re-layouts  19 us
    all_to_all x4, starting transfers between devices, on_device(): returned = lax.all_to_all(leaving, ring, split_axis=0, concat_axis=0)  18.3 us
    pallas_call x1, Pallas kernels, head(): pl.pallas_call(head_kernel, out_shape=(shape, shape), grid=(width // colu...  14.9 us
    reshape x1, local copies, waits for them, and re-layouts, on_device(): filter_spec.reshape(2, channels, count_three, count_two, count_one // SLA...  12.8 us
    ppermute x4, waiting for transfers between devices, project(): lax.ppermute(gated_mix, 'chan', [(i, (i + k) % count) for i in range(coun...  11.9 us
  transfers between devices with their start and end apart: 10, of which 5 were waited for; matrix products, arithmetic and copies ran while one was open for 28% of the time, Pallas kernels for 14%

profile of v3, /device:TPU:0, one launch (start us, length us, event | category | flops | bytes accessed | tf_op | source)
XLA Modules:
  0.0 214.6 jit_solution(8042205006336348128)
XLA Ops:
  0.0 1.0 slice.15
  1.0 2.4 %collective-permute-start = (bf16[3,128,2]{2,1,0:T(8,128)(2,1)S(1)}, bf16[3,128,2]{2,1,0:T(8,128)(2,1)S(1)}, u32[]{:S(2)}, u32[]{:S(2)}) collective-permute-start(bf16[3,128,2]{2,1,0:T(8,128)(2,1)S(1)} %slice.15), channel_id=1, source_target_pairs={{0,1},{1,4},{4,5},{5,8},{8,9},{9,12},{12,13},{13,16},{16,17},{17,2... | collective-permute-start | bytes 4616 | tf_op jit(solution)/shard_map/ppermute | solution.py:21
  3.4 7.4 %fusion.order = bf16[2048,2048]{1,0:T(8,128)(2,1)} fusion(s32[2048]{0:T(1024)S(1)} %add_bitcast_fusion), kind=kLoop, calls=%fused_computation.1 | loop fusion | flops 8388608 | bytes 8396800 | tf_op jit(solution)/shard_map/convert_element_type | solution.py:191
  10.9 0.7 copy.30
  11.6 0.7 pad.26.halo
  12.3 14.9 %gate_and_reorder.1 = (bf16[128,8192]{1,0:T(8,128)(2,1)}, bf16[128,8192]{1,0:T(8,128)(2,1)}) custom-call(bf16[3,128,128]{2,1,0:T(8,128)(2,1)} %pad.26.halo, f32[128,9]{1,0:T(8,128)} %bitcast.62, bf16[2048,2048]{1,0:T(8,128)(2,1)} %fusion.order, bf16[3,128,8192]{2,1,0:T(8,128)(2,1)} %block.9), custom_call_target="tpu_custom_call" | custom-call | flops 4294967296 | bytes 16777216 | tf_op jit(solution)/shard_map/gate_and_reorder/pallas_call | solution.py:232
  27.2 7.2 %all-to-all-start = ((bf16[16,8,8192]{2,1,0:T(8,128)(2,1)}), bf16[16,8,8192]{2,1,0:T(8,128)(2,1)S(1)}, u32[]{:S(2)}, u32[]{:S(2)}) async-start(bf16[16,8,8192]{2,1,0:T(8,128)(2,1)} %bitcast.58), calls=%async_computation | async-start | bytes 4194304 | tf_op jit(solution)/shard_map/all_to_all | solution.py:345
  34.4 12.8 %reshape.272 = bf16[2,8,8,112,4,16]{5,4,3,2,1,0:T(4,128)(2,1)} reshape(bf16[2,8,8,7168]{3,2,1,0:T(8,128)(2,1)} %param.11) | data formatting | bytes 3670016 | tf_op jit(solution)/shard_map/reshape | solution.py:350
  47.3 18.2 %copy.41 = bf16[2,8,4,8,16,112]{5,4,3,2,1,0:T(8,128)(2,1)} copy(bf16[2,8,4,8,16,112]{4,2,5,3,1,0:T(4,128)(2,1)} %bitcast.53) | data formatting | bytes 3670016
  65.4 3.7 %pad.27.clone = bf16[2,8,4,8,16,128]{5,4,3,2,1,0:T(8,128)(2,1)} pad(bf16[2,8,4,8,16,112]{5,4,3,2,1,0:T(8,128)(2,1)} %copy.41, bf16[]{:T(256)} %constant.141.clone.1), padding=0_0x0_0x0_0x0_0x0_0x0_16 | pad | bytes 3932162 | tf_op jit(solution)/shard_map/jit(_pad)/pad | solution.py:43
  69.3 0.3 multiply_convert_fusion
  69.8 0.1 multiply_convert_fusion.11
  69.9 0.1 broadcast_multiply_fusion.3
  70.0 0.5 mul.404
  70.5 0.5 mul.399
  71.0 0.1 broadcast_multiply_fusion
  71.2 0.3 mul.414
  71.5 0.3 mul.418
  71.9 0.3 multiply_convert_fusion.2
  72.3 3.3 %sine_multiply_fusion = (f32[4,256,128]{2,1,0:T(8,128)}, f32[4,256,128]{2,1,0:T(8,128)}) fusion(s32[256]{0:T(256)S(1)} %mul.383, s32[4,16,128]{2,1,0:T(8,128)S(1)} %broadcast_add_fusion), kind=kLoop, calls=%fused_computation.21 | loop fusion | flops 1966080 | bytes 1082368 | tf_op jit(solution)/shard_map/mul | solution.py:37
  75.6 0.2 fusion.47
  75.8 0.3 multiply_convert_fusion.5
  76.1 0.7 pad_maximum_fusion.3.undo_first
  76.8 0.6 pad_maximum_fusion.2.first
  77.5 0.7 pad_maximum_fusion.1.third
  78.1 0.7 maximum_maximum_fusion.1.second
  78.8 0.7 maximum_maximum_fusion.2.undo_second
  79.5 0.7 maximum_maximum_fusion.undo_third
  80.2 0.9 sine_multiply_fusion.1
  81.1 2.5 %copy.43 = bf16[16,8,8192]{2,0,1:T(8,128)(2,1)} copy(bf16[16,8,8192]{2,1,0:T(8,128)(2,1)S(1)} %all-to-all-done) | data formatting | bytes 4194304 | tf_op jit(solution)/shard_map/all_to_all | solution.py:345
  83.6 27.4 %spectral_conv.1 = bf16[8,16,8192]{2,1,0:T(8,128)(2,1)} custom-call(bf16[8,16,8192]{2,1,0:T(8,128)(2,1)} %bitcast.61, bf16[2,8,4,128,128]{4,3,2,1,0:T(8,128)(2,1)} %bitcast.59, bf16[128,64]{1,0:T(8,128)(2,1)} %pad_maximum_fusion.2.first, f32[64,128]{1,0:T(8,128)} %get-tuple-element.39.one_re, f32[64,128]{1,0:T(8,128)} %get-tuple-element.38.one_im, ...), custom_call_target="tpu_custom_call" | custom-call | flops 3200000000 | bytes 8388608 | tf_op jit(solution)/shard_map/spectral_conv/pallas_call | solution.py:165
  111.0 1.7 fusion.71
  112.7 1.1 copy.35
  113.8 6.0 %all-to-all-start.2 = ((bf16[16,8,2048]{2,1,0:T(8,128)(2,1)}), bf16[16,8,2048]{2,1,0:T(8,128)(2,1)S(1)}, u32[]{:S(2)}, u32[]{:S(2)}) async-start(bf16[16,8,2048]{2,1,0:T(8,128)(2,1)} %copy.35), calls=%async_computation.2 | async-start | bytes 1048576 | tf_op jit(solution)/shard_map/all_to_all | solution.py:366
  119.8 1.1 copy.33
  120.9 13.4 %all-to-all-done.2 = bf16[16,8,2048]{2,1,0:T(8,128)(2,1)S(1)} async-done(((bf16[16,8,2048]{2,1,0:T(8,128)(2,1)}), bf16[16,8,2048]{2,1,0:T(8,128)(2,1)S(1)}, u32[]{:S(2)}, u32[]{:S(2)}) %all-to-all-start.2) | async-done | bytes 524320 | tf_op jit(solution)/shard_map/all_to_all | solution.py:366
  134.2 4.1 %all-to-all-start.1 = ((bf16[16,8,2048]{2,1,0:T(8,128)(2,1)}), bf16[16,8,2048]{2,1,0:T(8,128)(2,1)S(1)}, u32[]{:S(2)}, u32[]{:S(2)}) async-start(bf16[16,8,2048]{2,1,0:T(8,128)(2,1)} %copy.33), calls=%async_computation.1 | async-start | bytes 1048576 | tf_op jit(solution)/shard_map/all_to_all | solution.py:366
  138.4 0.7 copy.34.skip
  139.1 7.6 %reorder_and_mix.5 = bf16[128,2048]{1,0:T(8,128)(2,1)} custom-call(bf16[3,128,128]{2,1,0:T(8,128)(2,1)} %pad.26.halo, f32[128,9]{1,0:T(8,128)} %bitcast.63, f32[128,1]{1,0:T(8,128)} %copy.34.skip, bf16[2048,2048]{1,0:T(8,128)(2,1)} %fusion.order, bf16[3,128,8192]{2,1,0:T(8,128)(2,1)} %block.9, bf16[3,128,8192]{2,1,0:T(8,128)(2,1)} %block.9, ...), custom_call_target="tpu_custom_call" | custom-call | flops 1073741824 | bytes 12582912 | tf_op jit(solution)/shard_map/reorder_and_mix/pallas_call | solution.py:266
  146.7 1.1 copy.39
  147.8 5.0 %all-to-all-done.1 = bf16[16,8,2048]{2,1,0:T(8,128)(2,1)S(1)} async-done(((bf16[16,8,2048]{2,1,0:T(8,128)(2,1)}), bf16[16,8,2048]{2,1,0:T(8,128)(2,1)S(1)}, u32[]{:S(2)}, u32[]{:S(2)}) %all-to-all-start.1) | async-done | bytes 524320 | tf_op jit(solution)/shard_map/all_to_all | solution.py:366
  152.8 4.1 %all-to-all-start.4 = ((bf16[16,8,2048]{2,1,0:T(8,128)(2,1)}), bf16[16,8,2048]{2,1,0:T(8,128)(2,1)S(1)}, u32[]{:S(2)}, u32[]{:S(2)}) async-start(bf16[16,8,2048]{2,1,0:T(8,128)(2,1)} %copy.39), calls=%async_computation.4 | async-start | bytes 1048576 | tf_op jit(solution)/shard_map/all_to_all | solution.py:366
  156.9 1.6 collective-permute-start.2
  158.5 7.6 %reorder_and_mix.4 = bf16[128,2048]{1,0:T(8,128)(2,1)} custom-call(bf16[3,128,128]{2,1,0:T(8,128)(2,1)} %pad.26.halo, f32[128,9]{1,0:T(8,128)} %bitcast.64, f32[128,1]{1,0:T(8,128)} %copy.34.skip, bf16[2048,2048]{1,0:T(8,128)(2,1)} %fusion.order, bf16[3,128,8192]{2,1,0:T(8,128)(2,1)} %block.9, bf16[3,128,8192]{2,1,0:T(8,128)(2,1)} %block.9, ...), custom_call_target="tpu_custom_call" | custom-call | flops 1073741824 | bytes 12582912 | tf_op jit(solution)/shard_map/reorder_and_mix/pallas_call | solution.py:266
  166.1 0.5 collective-permute-start.1
  166.7 1.1 copy.37
  167.7 3.6 %all-to-all-done.4 = bf16[16,8,2048]{2,1,0:T(8,128)(2,1)S(1)} async-done(((bf16[16,8,2048]{2,1,0:T(8,128)(2,1)}), bf16[16,8,2048]{2,1,0:T(8,128)(2,1)S(1)}, u32[]{:S(2)}, u32[]{:S(2)}) %all-to-all-start.4) | async-done | bytes 524320 | tf_op jit(solution)/shard_map/all_to_all | solution.py:366
  171.4 4.1 %all-to-all-start.3 = ((bf16[16,8,2048]{2,1,0:T(8,128)(2,1)}), bf16[16,8,2048]{2,1,0:T(8,128)(2,1)S(1)}, u32[]{:S(2)}, u32[]{:S(2)}) async-start(bf16[16,8,2048]{2,1,0:T(8,128)(2,1)} %copy.37), calls=%async_computation.3 | async-start | bytes 1048576 | tf_op jit(solution)/shard_map/all_to_all | solution.py:366
  175.5 0.3 fusion.39
  175.8 0.3 fusion.2
  176.2 7.7 %reorder_and_mix.7 = bf16[128,2048]{1,0:T(8,128)(2,1)} custom-call(bf16[3,128,128]{2,1,0:T(8,128)(2,1)} %pad.26.halo, f32[128,9]{1,0:T(8,128)} %bitcast.65, f32[128,1]{1,0:T(8,128)} %copy.34.skip, bf16[2048,2048]{1,0:T(8,128)(2,1)} %fusion.order, bf16[3,128,8192]{2,1,0:T(8,128)(2,1)} %block.9, bf16[3,128,8192]{2,1,0:T(8,128)(2,1)} %block.9, ...), custom_call_target="tpu_custom_call" | custom-call | flops 1073741824 | bytes 12582912 | tf_op jit(solution)/shard_map/reorder_and_mix/pallas_call | solution.py:266
  183.9 1.5 collective-permute-start.4
  185.4 0.3 fusion.41
  185.7 0.3 fusion.1
  186.0 3.9 %all-to-all-done.3 = bf16[16,8,2048]{2,1,0:T(8,128)(2,1)S(1)} async-done(((bf16[16,8,2048]{2,1,0:T(8,128)(2,1)}), bf16[16,8,2048]{2,1,0:T(8,128)(2,1)S(1)}, u32[]{:S(2)}, u32[]{:S(2)}) %all-to-all-start.3) | async-done | bytes 524320 | tf_op jit(solution)/shard_map/all_to_all | solution.py:366
  190.0 0.8 copy-done.7
  190.8 7.7 %reorder_and_mix.6 = bf16[128,2048]{1,0:T(8,128)(2,1)} custom-call(bf16[3,128,128]{2,1,0:T(8,128)(2,1)} %pad.26.halo, f32[128,9]{1,0:T(8,128)} %bitcast.66, f32[128,1]{1,0:T(8,128)} %copy.34.skip, bf16[2048,2048]{1,0:T(8,128)(2,1)} %fusion.order, bf16[3,128,8192]{2,1,0:T(8,128)(2,1)} %block.9, bf16[3,128,8192]{2,1,0:T(8,128)(2,1)} %block.9, ...), custom_call_target="tpu_custom_call" | custom-call | flops 1073741824 | bytes 12582912 | tf_op jit(solution)/shard_map/reorder_and_mix/pallas_call | solution.py:266
  198.4 1.5 collective-permute-start.3
  199.9 0.3 fusion.35
  200.3 0.3 fusion.4
  200.6 11.9 %collective-permute-done.3 = bf16[128,2048]{1,0:T(8,128)(2,1)S(1)} collective-permute-done((bf16[128,2048]{1,0:T(8,128)(2,1)}, bf16[128,2048]{1,0:T(8,128)(2,1)S(1)}, u32[]{:S(2)}, u32[]{:S(2)}) %collective-permute-start.3) | collective-permute-done | bytes 524320 | tf_op jit(solution)/shard_map/ppermute | solution.py:297
  212.5 0.3 fusion.37
  212.8 0.3 fusion.3
  213.2 1.5 pad_maximum_fusion
  (47 shorter events, 0.5 us)
Async XLA Ops:
  0.0 175.5 %copy-start = (bf16[256,128]{1,0:T(8,128)(2,1)S(1)}, bf16[256,128]{1,0:T(8,128)(2,1)}, u32[]{:S(2)}) copy-start(bf16[256,128]{1,0:T(8,128)(2,1)} %param.15) | copy-start | bytes 196612
  1.0 10.6 %collective-permute-start = (bf16[3,128,2]{2,1,0:T(8,128)(2,1)S(1)}, bf16[3,128,2]{2,1,0:T(8,128)(2,1)S(1)}, u32[]{:S(2)}, u32[]{:S(2)}) collective-permute-start(bf16[3,128,2]{2,1,0:T(8,128)(2,1)S(1)} %slice.15), channel_id=1, source_target_pairs={{0,1},{1,4},{4,5},{5,8},{8,9},{9,12},{12,13},{13,16},{16,17},{17,2... | collective-permute-start | bytes 4616 | tf_op jit(solution)/shard_map/ppermute | solution.py:21
  3.4 7.5 %copy-start.10 = (f32[3,3,128]{2,1,0:T(4,128)S(1)}, f32[3,3,128]{2,1,0:T(4,128)}, u32[]{:S(2)}) copy-start(f32[3,3,128]{2,1,0:T(4,128)} %param.9) | copy-start | bytes 13828
  27.2 53.9 %all-to-all-start = ((bf16[16,8,8192]{2,1,0:T(8,128)(2,1)}), bf16[16,8,8192]{2,1,0:T(8,128)(2,1)S(1)}, u32[]{:S(2)}, u32[]{:S(2)}) async-start(bf16[16,8,8192]{2,1,0:T(8,128)(2,1)} %bitcast.58), calls=%async_computation | async-start | bytes 4194304 | tf_op jit(solution)/shard_map/all_to_all | solution.py:345
  65.4 3.8 %copy-start.11 = (s32[112]{0:T(128)S(1)}, s32[112]{0:T(128)}, u32[]{:S(2)}) copy-start(s32[112]{0:T(128)} %param.13) | copy-start | bytes 1348
  65.4 4.2 %copy-start.9 = (s32[64]{0:T(128)S(1)}, s32[64]{0:T(128)}, u32[]{:S(2)}) copy-start(s32[64]{0:T(128)} %param.12) | copy-start | bytes 772
  65.4 4.3 %copy-start.12 = (s32[8]{0:T(128)S(1)}, s32[8]{0:T(128)}, u32[]{:S(2)}) copy-start(s32[8]{0:T(128)} %param.14) | copy-start | bytes 100
  112.7 25.7 %copy-start.13 = (f32[128]{0:T(128)S(1)}, f32[128]{0:T(128)}, u32[]{:S(2)}) copy-start(f32[128]{0:T(128)} %param.10) | copy-start | bytes 1540
  113.8 20.5 %all-to-all-start.2 = ((bf16[16,8,2048]{2,1,0:T(8,128)(2,1)}), bf16[16,8,2048]{2,1,0:T(8,128)(2,1)S(1)}, u32[]{:S(2)}, u32[]{:S(2)}) async-start(bf16[16,8,2048]{2,1,0:T(8,128)(2,1)} %copy.35), calls=%async_computation.2 | async-start | bytes 1048576 | tf_op jit(solution)/shard_map/all_to_all | solution.py:366
  134.2 4.9 %copy-start.8 = (bf16[16,8,2048]{2,1,0:T(8,128)(2,1)}, bf16[16,8,2048]{2,1,0:T(8,128)(2,1)S(1)}, u32[]{:S(2)}) copy-start(bf16[16,8,2048]{2,1,0:T(8,128)(2,1)S(1)} %all-to-all-done.2) | copy-start | bytes 1572868
  134.2 18.6 %all-to-all-start.1 = ((bf16[16,8,2048]{2,1,0:T(8,128)(2,1)}), bf16[16,8,2048]{2,1,0:T(8,128)(2,1)S(1)}, u32[]{:S(2)}, u32[]{:S(2)}) async-start(bf16[16,8,2048]{2,1,0:T(8,128)(2,1)} %copy.33), calls=%async_computation.1 | async-start | bytes 1048576 | tf_op jit(solution)/shard_map/all_to_all | solution.py:366
  146.7 10.2 %copy-start.1 = (bf16[128,2048]{1,0:T(8,128)(2,1)S(1)}, bf16[128,2048]{1,0:T(8,128)(2,1)}, u32[]{:S(2)}) copy-start(bf16[128,2048]{1,0:T(8,128)(2,1)} %reorder_and_mix.5) | copy-start | bytes 1572868
  152.8 5.7 %copy-start.6 = (bf16[16,8,2048]{2,1,0:T(8,128)(2,1)}, bf16[16,8,2048]{2,1,0:T(8,128)(2,1)S(1)}, u32[]{:S(2)}) copy-start(bf16[16,8,2048]{2,1,0:T(8,128)(2,1)S(1)} %all-to-all-done.1) | copy-start | bytes 1572868
  152.8 18.6 %all-to-all-start.4 = ((bf16[16,8,2048]{2,1,0:T(8,128)(2,1)}), bf16[16,8,2048]{2,1,0:T(8,128)(2,1)S(1)}, u32[]{:S(2)}, u32[]{:S(2)}) async-start(bf16[16,8,2048]{2,1,0:T(8,128)(2,1)} %copy.39), calls=%async_computation.4 | async-start | bytes 1048576 | tf_op jit(solution)/shard_map/all_to_all | solution.py:366
  156.9 18.6 %collective-permute-start.2 = (bf16[128,2048]{1,0:T(8,128)(2,1)S(1)}, bf16[128,2048]{1,0:T(8,128)(2,1)S(1)}, u32[]{:S(2)}, u32[]{:S(2)}) collective-permute-start(bf16[128,2048]{1,0:T(8,128)(2,1)S(1)} %copy-done.1), channel_id=1, source_target_pairs={{0,2},{2,0},{1,3},{3,1},{4,6},{6,4},{5,7},{7,5},{8,10},{10,8},{9,1... | collective-permute-start | bytes 1572872 | tf_op jit(solution)/shard_map/ppermute | solution.py:297
  166.1 19.2 %collective-permute-start.1 = (bf16[128,2048]{1,0:T(8,128)(2,1)}, bf16[128,2048]{1,0:T(8,128)(2,1)S(1)}, u32[]{:S(2)}, u32[]{:S(2)}) collective-permute-start(bf16[128,2048]{1,0:T(8,128)(2,1)} %reorder_and_mix.4), channel_id=1, source_target_pairs={{0,2},{2,0},{1,3},{3,1},{4,6},{6,4},{5,7},{7,5},{8,10},{10,8},{9,1... | collective-permute-start | bytes 1572872 | tf_op jit(solution)/shard_map/ppermute | solution.py:297
  171.4 4.8 %copy-start.5 = (bf16[16,8,2048]{2,1,0:T(8,128)(2,1)}, bf16[16,8,2048]{2,1,0:T(8,128)(2,1)S(1)}, u32[]{:S(2)}) copy-start(bf16[16,8,2048]{2,1,0:T(8,128)(2,1)S(1)} %all-to-all-done.4) | copy-start | bytes 1572868
  171.4 18.6 %all-to-all-start.3 = ((bf16[16,8,2048]{2,1,0:T(8,128)(2,1)}), bf16[16,8,2048]{2,1,0:T(8,128)(2,1)S(1)}, u32[]{:S(2)}, u32[]{:S(2)}) async-start(bf16[16,8,2048]{2,1,0:T(8,128)(2,1)} %copy.37), calls=%async_computation.3 | async-start | bytes 1048576 | tf_op jit(solution)/shard_map/all_to_all | solution.py:366
  176.2 9.5 %copy-start.2 = (bf16[128,2048]{1,0:T(8,128)(2,1)S(1)}, bf16[128,2048]{1,0:T(8,128)(2,1)}, u32[]{:S(2)}) copy-start(bf16[128,2048]{1,0:T(8,128)(2,1)} %reorder_and_mix.4) | copy-start | bytes 1572868
  183.9 16.1 %collective-permute-start.4 = (bf16[128,2048]{1,0:T(8,128)(2,1)}, bf16[128,2048]{1,0:T(8,128)(2,1)S(1)}, u32[]{:S(2)}, u32[]{:S(2)}) collective-permute-start(bf16[128,2048]{1,0:T(8,128)(2,1)} %reorder_and_mix.7), channel_id=1, source_target_pairs={{0,2},{2,0},{1,3},{3,1},{4,6},{6,4},{5,7},{7,5},{8,10},{10,8},{9,1... | collective-permute-start | bytes 1572872 | tf_op jit(solution)/shard_map/ppermute | solution.py:297
  190.0 0.8 copy-start.7
  190.8 9.5 %copy-start.3 = (bf16[128,2048]{1,0:T(8,128)(2,1)S(1)}, bf16[128,2048]{1,0:T(8,128)(2,1)}, u32[]{:S(2)}) copy-start(bf16[128,2048]{1,0:T(8,128)(2,1)} %reorder_and_mix.7) | copy-start | bytes 1572868
  198.4 14.1 %collective-permute-start.3 = (bf16[128,2048]{1,0:T(8,128)(2,1)}, bf16[128,2048]{1,0:T(8,128)(2,1)S(1)}, u32[]{:S(2)}, u32[]{:S(2)}) collective-permute-start(bf16[128,2048]{1,0:T(8,128)(2,1)} %reorder_and_mix.6), channel_id=1, source_target_pairs={{0,2},{2,0},{1,3},{3,1},{4,6},{6,4},{5,7},{7,5},{8,10},{10,8},{9,1... | collective-permute-start | bytes 1572872 | tf_op jit(solution)/shard_map/ppermute | solution.py:297
  200.3 12.6 %copy-start.4 = (bf16[128,2048]{1,0:T(8,128)(2,1)S(1)}, bf16[128,2048]{1,0:T(8,128)(2,1)}, u32[]{:S(2)}) copy-start(bf16[128,2048]{1,0:T(8,128)(2,1)} %reorder_and_mix.6) | copy-start | bytes 1572868

commit v4 on v2

--- a/solution.py
+++ b/solution.py
@@ -12,7 +12,6 @@
 B = 128
 LANES = 128
 SLAB = 16
-PARTS = 2
 
 
 def passed_along(value, axis, steps):
@@ -342,12 +341,17 @@
     conv_rows = convolve(rows, filt, tables, size_c)
 
     conv_out = jnp.swapaxes(conv_rows, 0, 1)
-    parts = PARTS if per_source % PARTS == 0 else 1
-    step = tokens_here // parts
+    quarter = tokens_here // 4
+    steps = (2 * quarter, quarter, quarter) if per_source % 4 == 0 else (tokens_here,)
     mixed = []
-    for part in range(parts):
-        span = slice(part * step, (part + 1) * step)
-        returned = lax.all_to_all(conv_out[:, :, span], ring, split_axis=0, concat_axis=0)
+    ready = []
+    for part, step in enumerate(steps):
+        start = sum(steps[:part])
+        span = slice(start, start + step)
+        leaving = conv_out[:, :, span]
+        if part >= 2:
+            leaving, _ = lax.optimization_barrier((leaving, ready[part - 2]))
+        returned = lax.all_to_all(leaving, ring, split_axis=0, concat_axis=0)
         returned = returned.reshape(sources * channels, step)
         if order is None:
             token_major = reordered(returned, size_c, True)
@@ -367,9 +371,10 @@
                 order,
                 gated_values,
                 returned,
-                part * (step // width),
+                start // width,
             )
-        mixed.append(project(out_weight, gated_mix))
+        ready.append(gated_mix)
+    mixed = [project(out_weight, gated_mix) for gated_mix in ready]
     return jnp.concatenate(mixed, axis=1)
 
 

time: 214 us -> 220 us (1.028)
  waiting for transfers between devices: 54.4 us -> 47.4 us
  starting transfers between devices: 25.4 us -> 31 us
  Pallas kernels: 63.2 us -> 67.2 us
  local copies, waits for them, and re-layouts: 48.1 us -> 50.4 us
    ppermute x2 -> x3, waiting for transfers between devices: 23.4 us -> 10.4 us  [project(): lax.ppermute(gated_mix, 'chan', [(i, (i + k) % count) for i in range(coun...]
    all_to_all x2 -> x3, waiting for transfers between devices: 31 us -> 37 us  [on_device(): returned = lax.all_to_all(leaving, ring, split_axis=0, concat_axis=0)]
    pallas_call x2 -> x3, Pallas kernels: 22.1 us -> 26.3 us  [tail(): pl.pallas_call(functools.partial(tail_kernel, base), out_shape=jax.ShapeD...]
    all_to_all x2 -> x3, starting transfers between devices: 12.9 us -> 17 us  [on_device(): returned = lax.all_to_all(leaving, ring, split_axis=0, concat_axis=0)]
    unnamed x21 -> x25, local copies, waits for them, and re-layouts: 19.2 us -> 20 us
    slice x3 -> x4, local copies, waits for them, and re-layouts: 4.8 us -> 5.21 us  [on_device(): leaving = conv_out[:, :, span]]
  transfers between devices with their start and end apart: 6 -> 8, of which waited for: 4 -> 5; matrix products, arithmetic and copies ran while one was open for 27% -> 28% of each run, Pallas kernels for 10% -> 12%
where the time goes in v4:
time: 220 us; the launch traced here: 219 us
  Pallas kernels  67.2 us (31%)
  local copies, waits for them, and re-layouts  50.4 us (23%)
  waiting for transfers between devices  47.4 us (22%)
  starting transfers between devices  31 us (14%)
  other arithmetic  18.8 us (9%)
  matrix products  3.48 us (2%)
    all_to_all x3, waiting for transfers between devices, on_device(): returned = lax.all_to_all(leaving, ring, split_axis=0, concat_axis=0)  37 us
    pallas_call x1, Pallas kernels, convolve(): pl.pallas_call(functools.partial(conv_kernel, size_c), out_shape=jax.Shap...  27.4 us
    pallas_call x3, Pallas kernels, tail(): pl.pallas_call(functools.partial(tail_kernel, base), out_shape=jax.ShapeD...  26.3 us
    unnamed x25, local copies, waits for them, and re-layouts  20 us
    all_to_all x3, starting transfers between devices, on_device(): returned = lax.all_to_all(leaving, ring, split_axis=0, concat_axis=0)  17 us
    pallas_call x1, Pallas kernels, head(): pl.pallas_call(head_kernel, out_shape=(shape, shape), grid=(tokens // wid...  13.6 us
    reshape x1, local copies, waits for them, and re-layouts, on_device(): filter_spec.reshape(2, channels, count_three, count_two, count_one // SLA...  12.8 us
    ppermute x3, waiting for transfers between devices, project(): lax.ppermute(gated_mix, 'chan', [(i, (i + k) % count) for i in range(coun...  10.4 us
  transfers between devices with their start and end apart: 8, of which 5 were waited for; matrix products, arithmetic and copies ran while one was open for 28% of the time, Pallas kernels for 12%

profile of v4, /device:TPU:0, one launch (start us, length us, event | category | flops | bytes accessed | tf_op | source)
XLA Modules:
  0.0 218.6 jit_solution(13517128607819187770)
XLA Ops:
  0.0 1.0 slice.12
  1.0 2.4 %collective-permute-start = (bf16[3,128,2]{2,1,0:T(8,128)(2,1)S(1)}, bf16[3,128,2]{2,1,0:T(8,128)(2,1)S(1)}, u32[]{:S(2)}, u32[]{:S(2)}) collective-permute-start(bf16[3,128,2]{2,1,0:T(8,128)(2,1)S(1)} %slice.12), channel_id=1, source_target_pairs={{0,1},{1,4},{4,5},{5,8},{8,9},{9,12},{12,13},{13,16},{16,17},{17,2... | collective-permute-start | bytes 4616 | tf_op jit(solution)/shard_map/ppermute | solution.py:20
  3.4 7.4 %fusion.order = bf16[2048,2048]{1,0:T(8,128)(2,1)} fusion(s32[2048]{0:T(1024)S(1)} %add_bitcast_fusion), kind=kLoop, calls=%fused_computation.1 | loop fusion | flops 8388608 | bytes 8396800 | tf_op jit(solution)/shard_map/convert_element_type | solution.py:190
  10.9 0.7 copy.26
  11.6 0.7 pad.26.halo
  12.4 13.6 %gate_and_reorder.1 = (bf16[128,8192]{1,0:T(8,128)(2,1)}, bf16[128,8192]{1,0:T(8,128)(2,1)}) custom-call(bf16[3,128,128]{2,1,0:T(8,128)(2,1)} %pad.26.halo, f32[128,9]{1,0:T(8,128)} %bitcast.59, bf16[2048,2048]{1,0:T(8,128)(2,1)} %fusion.order, bf16[3,128,8192]{2,1,0:T(8,128)(2,1)} %block.7, bf16[3,128,8192]{2,1,0:T(8,128)(2,1)} %block.7), custom_call_target="tpu_custom_call" | custom-call | flops 4294967296 | bytes 16777216 | tf_op jit(solution)/shard_map/gate_and_reorder/pallas_call | solution.py:217
  26.0 7.3 %all-to-all-start = ((bf16[16,8,8192]{2,1,0:T(8,128)(2,1)}), bf16[16,8,8192]{2,1,0:T(8,128)(2,1)S(1)}, u32[]{:S(2)}, u32[]{:S(2)}) async-start(bf16[16,8,8192]{2,1,0:T(8,128)(2,1)} %bitcast.54), calls=%async_computation | async-start | bytes 4194304 | tf_op jit(solution)/shard_map/all_to_all | solution.py:332
  33.3 12.8 %reshape.263 = bf16[2,8,8,112,4,16]{5,4,3,2,1,0:T(4,128)(2,1)} reshape(bf16[2,8,8,7168]{3,2,1,0:T(8,128)(2,1)} %param.11) | data formatting | bytes 3670016 | tf_op jit(solution)/shard_map/reshape | solution.py:337
  46.1 18.2 %copy.35 = bf16[2,8,4,8,16,112]{5,4,3,2,1,0:T(8,128)(2,1)} copy(bf16[2,8,4,8,16,112]{4,2,5,3,1,0:T(4,128)(2,1)} %bitcast.50) | data formatting | bytes 3670016
  64.2 3.7 %pad.27.clone = bf16[2,8,4,8,16,128]{5,4,3,2,1,0:T(8,128)(2,1)} pad(bf16[2,8,4,8,16,112]{5,4,3,2,1,0:T(8,128)(2,1)} %copy.35, bf16[]{:T(256)} %constant.137.clone.1), padding=0_0x0_0x0_0x0_0x0_0x0_16 | pad | bytes 3932162 | tf_op jit(solution)/shard_map/jit(_pad)/pad | solution.py:42
  68.0 0.1 reshape.268
  68.0 0.3 multiply_convert_fusion
  68.4 0.1 mul.381
  68.4 0.1 add.165
  68.5 0.1 multiply_convert_fusion.11
  68.7 0.1 broadcast_multiply_fusion.3
  68.8 0.5 mul.402
  69.3 0.5 mul.397
  69.8 0.1 broadcast_multiply_fusion
  70.0 0.3 mul.412
  70.3 0.3 mul.416
  70.7 0.3 multiply_convert_fusion.2
  71.0 0.1 broadcast_add_fusion
  71.1 3.2 %sine_multiply_fusion = (f32[4,256,128]{2,1,0:T(8,128)}, f32[4,256,128]{2,1,0:T(8,128)}) fusion(s32[256]{0:T(256)S(1)} %mul.381, s32[4,16,128]{2,1,0:T(8,128)S(1)} %broadcast_add_fusion), kind=kLoop, calls=%fused_computation.19 | loop fusion | flops 1966080 | bytes 1082368 | tf_op jit(solution)/shard_map/mul | solution.py:36
  74.3 0.2 fusion.43
  74.5 0.3 multiply_convert_fusion.5
  74.9 0.7 pad_maximum_fusion.3.undo_first
  75.6 0.6 pad_maximum_fusion.2.first
  76.2 0.7 pad_maximum_fusion.1.third
  76.9 0.7 maximum_maximum_fusion.1.second
  77.5 0.7 maximum_maximum_fusion.2.undo_second
  78.2 0.7 maximum_maximum_fusion.undo_third
  78.9 0.8 sine_multiply_fusion.1
  79.8 2.5 %copy.37 = bf16[16,8,8192]{2,0,1:T(8,128)(2,1)} copy(bf16[16,8,8192]{2,1,0:T(8,128)(2,1)S(1)} %all-to-all-done) | data formatting | bytes 4194304 | tf_op jit(solution)/shard_map/all_to_all | solution.py:332
  82.3 27.4 %spectral_conv.1 = bf16[8,16,8192]{2,1,0:T(8,128)(2,1)} custom-call(bf16[8,16,8192]{2,1,0:T(8,128)(2,1)} %bitcast.58, bf16[2,8,4,128,128]{4,3,2,1,0:T(8,128)(2,1)} %bitcast.55, bf16[128,64]{1,0:T(8,128)(2,1)} %pad_maximum_fusion.2.first, f32[64,128]{1,0:T(8,128)} %get-tuple-element.35.one_re, f32[64,128]{1,0:T(8,128)} %get-tuple-element.34.one_im, ...), custom_call_target="tpu_custom_call" | custom-call | flops 3200000000 | bytes 8388608 | tf_op jit(solution)/shard_map/spectral_conv/pallas_call | solution.py:164
  109.7 1.3 fusion.65
  111.0 1.1 copy.31
  112.0 6.0 %all-to-all-start.2 = ((bf16[16,8,2048]{2,1,0:T(8,128)(2,1)}), bf16[16,8,2048]{2,1,0:T(8,128)(2,1)S(1)}, u32[]{:S(2)}, u32[]{:S(2)}) async-start(bf16[16,8,2048]{2,1,0:T(8,128)(2,1)} %copy.31), calls=%async_computation.2 | async-start | bytes 1048576 | tf_op jit(solution)/shard_map/all_to_all | solution.py:354
  118.1 1.3 slice.16
  119.4 1.6 copy.29
  120.9 11.6 %all-to-all-done.2 = bf16[16,8,2048]{2,1,0:T(8,128)(2,1)S(1)} async-done(((bf16[16,8,2048]{2,1,0:T(8,128)(2,1)}), bf16[16,8,2048]{2,1,0:T(8,128)(2,1)S(1)}, u32[]{:S(2)}, u32[]{:S(2)}) %all-to-all-start.2) | async-done | bytes 524320 | tf_op jit(solution)/shard_map/all_to_all | solution.py:354
  132.5 4.1 %all-to-all-start.1 = ((bf16[16,8,4096]{2,1,0:T(8,128)(2,1)}), bf16[16,8,4096]{2,1,0:T(8,128)(2,1)S(1)}, u32[]{:S(2)}, u32[]{:S(2)}) async-start(bf16[16,8,4096]{2,1,0:T(8,128)(2,1)} %copy.29), calls=%async_computation.1 | async-start | bytes 2097152 | tf_op jit(solution)/shard_map/all_to_all | solution.py:354
  136.7 0.7 copy.30.skip
  137.4 7.6 %reorder_and_mix.4 = bf16[128,2048]{1,0:T(8,128)(2,1)} custom-call(bf16[3,128,128]{2,1,0:T(8,128)(2,1)} %pad.26.halo, f32[128,9]{1,0:T(8,128)} %bitcast.60, f32[128,1]{1,0:T(8,128)} %copy.30.skip, bf16[2048,2048]{1,0:T(8,128)(2,1)} %fusion.order, bf16[3,128,8192]{2,1,0:T(8,128)(2,1)} %block.7, bf16[3,128,8192]{2,1,0:T(8,128)(2,1)} %block.7, ...), custom_call_target="tpu_custom_call" | custom-call | flops 1073741824 | bytes 12582912 | tf_op jit(solution)/shard_map/reorder_and_mix/pallas_call | solution.py:253
  145.0 1.5 collective-permute-start.2
  146.5 13.1 %all-to-all-done.1 = bf16[16,8,4096]{2,1,0:T(8,128)(2,1)S(1)} async-done(((bf16[16,8,4096]{2,1,0:T(8,128)(2,1)}), bf16[16,8,4096]{2,1,0:T(8,128)(2,1)S(1)}, u32[]{:S(2)}, u32[]{:S(2)}) %all-to-all-start.1) | async-done | bytes 1048608 | tf_op jit(solution)/shard_map/all_to_all | solution.py:354
  159.6 1.0 copy-done.2
  160.5 11.0 %reorder_and_mix.3 = bf16[128,4096]{1,0:T(8,128)(2,1)} custom-call(bf16[3,128,128]{2,1,0:T(8,128)(2,1)} %pad.26.halo, f32[128,9]{1,0:T(8,128)} %bitcast.61, f32[128,1]{1,0:T(8,128)} %copy.30.skip, bf16[2048,2048]{1,0:T(8,128)(2,1)} %fusion.order, bf16[3,128,8192]{2,1,0:T(8,128)(2,1)} %block.7, bf16[3,128,8192]{2,1,0:T(8,128)(2,1)} %block.7, ...), custom_call_target="tpu_custom_call" | custom-call | flops 2147483648 | bytes 12582912 | tf_op jit(solution)/shard_map/reorder_and_mix/pallas_call | solution.py:253
  171.6 1.1 copy.33
  172.6 6.9 %all-to-all-start.3 = ((bf16[16,8,2048]{2,1,0:T(8,128)(2,1)}), bf16[16,8,2048]{2,1,0:T(8,128)(2,1)S(1)}, u32[]{:S(2)}, u32[]{:S(2)}) async-start(bf16[16,8,2048]{2,1,0:T(8,128)(2,1)} %copy.33), calls=%async_computation.3 | async-start | bytes 1048576 | tf_op jit(solution)/shard_map/all_to_all | solution.py:354
  179.5 1.5 collective-permute-start.1
  181.0 0.3 fusion.36
  181.3 0.3 fusion.2
  181.7 12.3 %all-to-all-done.3 = bf16[16,8,2048]{2,1,0:T(8,128)(2,1)S(1)} async-done(((bf16[16,8,2048]{2,1,0:T(8,128)(2,1)}), bf16[16,8,2048]{2,1,0:T(8,128)(2,1)S(1)}, u32[]{:S(2)}, u32[]{:S(2)}) %all-to-all-start.3) | async-done | bytes 524320 | tf_op jit(solution)/shard_map/all_to_all | solution.py:354
  194.0 0.8 copy-done.5
  194.8 7.6 %reorder_and_mix.5 = bf16[128,2048]{1,0:T(8,128)(2,1)} custom-call(bf16[3,128,128]{2,1,0:T(8,128)(2,1)} %pad.26.halo, f32[128,9]{1,0:T(8,128)} %bitcast.62, f32[128,1]{1,0:T(8,128)} %copy.30.skip, bf16[2048,2048]{1,0:T(8,128)(2,1)} %fusion.order, bf16[3,128,8192]{2,1,0:T(8,128)(2,1)} %block.7, bf16[3,128,8192]{2,1,0:T(8,128)(2,1)} %block.7, ...), custom_call_target="tpu_custom_call" | custom-call | flops 1073741824 | bytes 12582912 | tf_op jit(solution)/shard_map/reorder_and_mix/pallas_call | solution.py:253
  202.4 1.4 collective-permute-start.3
  203.8 1.4 collective-permute-done.1
  205.2 1.7 fusion.38
  206.9 0.5 fusion.1
  207.4 9.1 %collective-permute-done.3 = bf16[128,2048]{1,0:T(8,128)(2,1)S(1)} collective-permute-done((bf16[128,2048]{1,0:T(8,128)(2,1)}, bf16[128,2048]{1,0:T(8,128)(2,1)S(1)}, u32[]{:S(2)}, u32[]{:S(2)}) %collective-permute-start.3) | collective-permute-done | bytes 524320 | tf_op jit(solution)/shard_map/ppermute | solution.py:284
  216.4 0.3 fusion.34
  216.8 0.3 fusion.3
  217.1 1.5 pad_maximum_fusion
  (36 shorter events, 0.2 us)
Async XLA Ops:
  0.0 181.0 %copy-start = (bf16[256,128]{1,0:T(8,128)(2,1)S(1)}, bf16[256,128]{1,0:T(8,128)(2,1)}, u32[]{:S(2)}) copy-start(bf16[256,128]{1,0:T(8,128)(2,1)} %param.15) | copy-start | bytes 196612
  1.0 10.6 %collective-permute-start = (bf16[3,128,2]{2,1,0:T(8,128)(2,1)S(1)}, bf16[3,128,2]{2,1,0:T(8,128)(2,1)S(1)}, u32[]{:S(2)}, u32[]{:S(2)}) collective-permute-start(bf16[3,128,2]{2,1,0:T(8,128)(2,1)S(1)} %slice.12), channel_id=1, source_target_pairs={{0,1},{1,4},{4,5},{5,8},{8,9},{9,12},{12,13},{13,16},{16,17},{17,2... | collective-permute-start | bytes 4616 | tf_op jit(solution)/shard_map/ppermute | solution.py:20
  3.4 7.4 %copy-start.8 = (f32[3,3,128]{2,1,0:T(4,128)S(1)}, f32[3,3,128]{2,1,0:T(4,128)}, u32[]{:S(2)}) copy-start(f32[3,3,128]{2,1,0:T(4,128)} %param.9) | copy-start | bytes 13828
  26.0 53.8 %all-to-all-start = ((bf16[16,8,8192]{2,1,0:T(8,128)(2,1)}), bf16[16,8,8192]{2,1,0:T(8,128)(2,1)S(1)}, u32[]{:S(2)}, u32[]{:S(2)}) async-start(bf16[16,8,8192]{2,1,0:T(8,128)(2,1)} %bitcast.54), calls=%async_computation | async-start | bytes 4194304 | tf_op jit(solution)/shard_map/all_to_all | solution.py:332
  64.2 3.8 %copy-start.9 = (s32[112]{0:T(128)S(1)}, s32[112]{0:T(128)}, u32[]{:S(2)}) copy-start(s32[112]{0:T(128)} %param.13) | copy-start | bytes 1348
  64.2 4.2 %copy-start.7 = (s32[64]{0:T(128)S(1)}, s32[64]{0:T(128)}, u32[]{:S(2)}) copy-start(s32[64]{0:T(128)} %param.12) | copy-start | bytes 772
  64.2 4.3 %copy-start.10 = (s32[8]{0:T(128)S(1)}, s32[8]{0:T(128)}, u32[]{:S(2)}) copy-start(s32[8]{0:T(128)} %param.14) | copy-start | bytes 100
  112.0 20.5 %all-to-all-start.2 = ((bf16[16,8,2048]{2,1,0:T(8,128)(2,1)}), bf16[16,8,2048]{2,1,0:T(8,128)(2,1)S(1)}, u32[]{:S(2)}, u32[]{:S(2)}) async-start(bf16[16,8,2048]{2,1,0:T(8,128)(2,1)} %copy.31), calls=%async_computation.2 | async-start | bytes 1048576 | tf_op jit(solution)/shard_map/all_to_all | solution.py:354
  119.4 17.3 %copy-start.11 = (f32[128]{0:T(128)S(1)}, f32[128]{0:T(128)}, u32[]{:S(2)}) copy-start(f32[128]{0:T(128)} %param.10) | copy-start | bytes 1540
  132.5 4.9 %copy-start.6 = (bf16[16,8,2048]{2,1,0:T(8,128)(2,1)}, bf16[16,8,2048]{2,1,0:T(8,128)(2,1)S(1)}, u32[]{:S(2)}) copy-start(bf16[16,8,2048]{2,1,0:T(8,128)(2,1)S(1)} %all-to-all-done.2) | copy-start | bytes 1572868
  132.5 27.0 %all-to-all-start.1 = ((bf16[16,8,4096]{2,1,0:T(8,128)(2,1)}), bf16[16,8,4096]{2,1,0:T(8,128)(2,1)S(1)}, u32[]{:S(2)}, u32[]{:S(2)}) async-start(bf16[16,8,4096]{2,1,0:T(8,128)(2,1)} %copy.29), calls=%async_computation.1 | async-start | bytes 2097152 | tf_op jit(solution)/shard_map/all_to_all | solution.py:354
  145.0 36.0 %collective-permute-start.2 = (bf16[128,2048]{1,0:T(8,128)(2,1)}, bf16[128,2048]{1,0:T(8,128)(2,1)S(1)}, u32[]{:S(2)}, u32[]{:S(2)}) collective-permute-start(bf16[128,2048]{1,0:T(8,128)(2,1)} %reorder_and_mix.4), channel_id=1, source_target_pairs={{0,2},{2,0},{1,3},{3,1},{4,6},{6,4},{5,7},{7,5},{8,10},{10,8},{9,1... | collective-permute-start | bytes 1572872 | tf_op jit(solution)/shard_map/ppermute | solution.py:284
  159.6 1.0 copy-start.2
  171.6 8.0 %copy-start.1 = (bf16[128,4096]{1,0:T(8,128)(2,1)S(1)}, bf16[128,4096]{1,0:T(8,128)(2,1)}, u32[]{:S(2)}) copy-start(bf16[128,4096]{1,0:T(8,128)(2,1)} %reorder_and_mix.3) | copy-start | bytes 3145732
  171.6 9.8 %copy-start.3 = (bf16[128,2048]{1,0:T(8,128)(2,1)S(1)}, bf16[128,2048]{1,0:T(8,128)(2,1)}, u32[]{:S(2)}) copy-start(bf16[128,2048]{1,0:T(8,128)(2,1)} %reorder_and_mix.4) | copy-start | bytes 1572868
  172.6 21.3 %all-to-all-start.3 = ((bf16[16,8,2048]{2,1,0:T(8,128)(2,1)}), bf16[16,8,2048]{2,1,0:T(8,128)(2,1)S(1)}, u32[]{:S(2)}, u32[]{:S(2)}) async-start(bf16[16,8,2048]{2,1,0:T(8,128)(2,1)} %copy.33), calls=%async_computation.3 | async-start | bytes 1048576 | tf_op jit(solution)/shard_map/all_to_all | solution.py:354
  179.5 25.7 %collective-permute-start.1 = (bf16[128,4096]{1,0:T(8,128)(2,1)S(1)}, bf16[128,4096]{1,0:T(8,128)(2,1)}, u32[]{:S(2)}, u32[]{:S(2)}) collective-permute-start(bf16[128,4096]{1,0:T(8,128)(2,1)S(1)} %copy-done.1), channel_id=1, source_target_pairs={{0,2},{2,0},{1,3},{3,1},{4,6},{6,4},{5,7},{7,5},{8,10},{10,8},{9,1... | collective-permute-start | bytes 3145736 | tf_op jit(solution)/shard_map/ppermute | solution.py:284
  194.0 0.8 copy-start.5
  202.4 14.0 %collective-permute-start.3 = (bf16[128,2048]{1,0:T(8,128)(2,1)}, bf16[128,2048]{1,0:T(8,128)(2,1)S(1)}, u32[]{:S(2)}, u32[]{:S(2)}) collective-permute-start(bf16[128,2048]{1,0:T(8,128)(2,1)} %reorder_and_mix.5), channel_id=1, source_target_pairs={{0,2},{2,0},{1,3},{3,1},{4,6},{6,4},{5,7},{7,5},{8,10},{10,8},{9,1... | collective-permute-start | bytes 1572872 | tf_op jit(solution)/shard_map/ppermute | solution.py:284
  206.9 9.9 %copy-start.4 = (bf16[128,2048]{1,0:T(8,128)(2,1)S(1)}, bf16[128,2048]{1,0:T(8,128)(2,1)}, u32[]{:S(2)}) copy-start(bf16[128,2048]{1,0:T(8,128)(2,1)} %reorder_and_mix.5) | copy-start | bytes 1572868
